TPU v7x, 32 devices: a whole 2x2x4 slice. The times are simulated.
32 devices in a mesh: dp: 8 (over z, x), tensor: 4 (over y, core).
Axes of the slice: x: 2, y: 2, z: 4, core: 2. Of those that a mesh axis runs over, the one named last changes fastest.
Arguments:
- inputs: bfloat16 [16, 256, 2048], P('dp', 'tensor'), may hold values from -36 to 36
- attn_norm: bfloat16 [2048], P('dp'), may hold values from 0.5 to 1.5
- query_weight: bfloat16 [2048, 1280], P('dp', 'tensor'), may hold values from -0.125 to 0.125
- key_value_weight: bfloat16 [2048, 640], P('dp'), may hold values from -0.125 to 0.125
- out_weight: bfloat16 [1280, 2048], P('tensor', 'dp'), may hold values from -0.625 to 0.625
- ffn_norm: bfloat16 [2048], P('dp'), may hold values from 0.5 to 1.5
- gate_weight: bfloat16 [2048, 2816], P('dp', 'tensor'), may hold values from -0.125 to 0.125
- up_weight: bfloat16 [2048, 2816], P('dp', 'tensor'), may hold values from -0.125 to 0.125
- down_weight: bfloat16 [2816, 2048], P('tensor', 'dp'), may hold values from -0.109375 to 0.109375
- query_gain: bfloat16 [64], replicated, may hold values from 0.099609375 to 1.8984375
- key_gain: bfloat16 [64], replicated, may hold values from 0.099609375 to 1.8984375
- cotangent: bfloat16 [16, 256, 2048], P('dp', 'tensor'), may hold values from -6 to 6
Outputs:
- output: bfloat16 [16, 256, 2048], P('dp', 'tensor')
- input_grad: float32 [16, 256, 2048], P('dp', 'tensor')
- attn_norm_grad: float32 [2048], P('dp')
- query_weight_grad: float32 [2048, 1280], P('dp', 'tensor')
- kv_weight_grad: float32 [2048, 640], P('dp')
- out_weight_grad: float32 [1280, 2048], P('tensor', 'dp')
- ffn_norm_grad: float32 [2048], P('dp')
- gate_weight_grad: float32 [2048, 2816], P('dp', 'tensor')
- up_weight_grad: float32 [2048, 2816], P('dp', 'tensor')
- down_weight_grad: float32 [2816, 2048], P('tensor', 'dp')
- query_gain_grad: float32 [64], replicated
- key_gain_grad: float32 [64], replicated
All inputs are finite; a program needn't handle non-finite values.
Results may differ from a plain program's by a relative error of at most 0.02.
Values may be sent and summed in bfloat16 or wider, within the bound.
No kernel may reach another device: no remote copies, remote signals or barrier semaphores. Data moves between devices by JAX's collectives and lax.ppermute only.
A program may use at most 128 MiB of HBM per device.

v0:
```python
from functools import partial

import jax
import jax.numpy as jnp
from jax import lax
from jax.sharding import PartitionSpec as P

norm_eps = 1e-06
rope_base = 10000.0
masked_score = -1e30


def rms_scale(value_tensors, gain):
    mean_square = jnp.mean(value_tensors * value_tensors, axis=-1, keepdims=True)
    return value_tensors * lax.rsqrt(mean_square + norm_eps) * gain


def rope_tables(token_length, head_size):
    half_size = head_size // 2
    inverse = rope_base ** (-2.0 * jnp.arange(half_size, dtype=jnp.float32) / head_size)
    angles = jnp.arange(token_length, dtype=jnp.float32)[:, None] * inverse[None, :]
    cosine = jnp.concatenate([jnp.cos(angles), jnp.cos(angles)], axis=-1)
    sine = jnp.concatenate([jnp.sin(angles), jnp.sin(angles)], axis=-1)
    return (cosine, sine)


def rotate(value_tensors, cosine, sine):
    half_size = value_tensors.shape[-1] // 2
    turned = jnp.concatenate(
        [-value_tensors[..., half_size:], value_tensors[..., :half_size]], axis=-1
    )
    return value_tensors * cosine[:, None, :] + turned * sine[:, None, :]


def head_prep(cosine, sine, pre_values, gain_values):
    return rotate(rms_scale(pre_values, gain_values), cosine, sine)


def gated_product(gate_in, upward_in):
    return jax.nn.silu(gate_in) * upward_in


def product(left, right):
    return jnp.dot(left, right, preferred_element_type=jnp.float32)


def left_transposed(left, right):
    return lax.dot_general(
        left, right, (((0,), (0,)), ((), ())), preferred_element_type=jnp.float32
    )


def right_transposed(left, right):
    return lax.dot_general(
        left, right, (((1,), (1,)), ((), ())), preferred_element_type=jnp.float32
    )


def collect(rows_low):
    return lax.all_gather(rows_low, "tensor", axis=0, tiled=True)


def spread(partial_term, row_count):
    return lax.psum_scatter(
        partial_term(jnp.int32(0), row_count * lax.axis_size("tensor")).astype(jnp.bfloat16),
        "tensor",
        scatter_dimension=0,
        tiled=True,
    ).astype(jnp.float32)


def fetch(
    attn_norm,
    query_weight,
    key_value_weight,
    out_weight,
    ffn_norm,
    gate_weight,
    up_weight,
    down_weight,
):
    return (
        lax.all_gather(attn_norm, "dp", axis=0, tiled=True),
        lax.all_gather(query_weight, "dp", axis=0, tiled=True),
        lax.all_gather(key_value_weight, "dp", axis=0, tiled=True),
        lax.all_gather(out_weight, "dp", axis=1, tiled=True),
        lax.all_gather(ffn_norm, "dp", axis=0, tiled=True),
        lax.all_gather(gate_weight, "dp", axis=0, tiled=True),
        lax.all_gather(up_weight, "dp", axis=0, tiled=True),
        lax.all_gather(down_weight, "dp", axis=1, tiled=True),
    )


def head_select(local_heads, kv_heads):
    total_heads = local_heads * lax.axis_size("tensor")
    group_size = total_heads // kv_heads
    global_heads = lax.axis_index("tensor") * local_heads + jnp.arange(local_heads, dtype=jnp.int32)
    return global_heads[:, None] // group_size == jnp.arange(kv_heads, dtype=jnp.int32)[None, :]


def attention_scores(queries, keys_local):
    token_length = queries.shape[0]
    raw_scores = jnp.einsum(
        "qhd,khd->hqk", queries, keys_local, preferred_element_type=jnp.float32
    ) * queries.shape[-1] ** (-0.5)
    causal = jnp.arange(token_length)[:, None] >= jnp.arange(token_length)[None, :]
    return jnp.where(causal[None], raw_scores, masked_score)


def forward_term(left, right):

    def partial_term(first_row, row_span):
        return product(left, right)

    return partial_term


def layer_forward(rows_in, full, query_gain, key_gain, tables, selector):
    (
        attn_norm,
        query_weight,
        key_value_weight,
        out_weight,
        ffn_norm,
        gate_weight,
        up_weight,
        down_weight,
    ) = full
    cosine, sine = tables
    head_size = query_gain.shape[0]
    local_heads = query_weight.shape[1] // head_size
    kv_heads = key_value_weight.shape[1] // (2 * head_size)
    row_count = rows_in.shape[0]
    tokens = rows_in.astype(jnp.float32)
    normed = rms_scale(tokens, attn_norm.astype(jnp.float32)).astype(jnp.bfloat16)
    whole = collect(normed)
    token_length = whole.shape[0]
    query_pre = product(whole, query_weight).reshape(token_length, local_heads, head_size)
    kv_pre = product(whole, key_value_weight)
    key_pre = kv_pre[:, : kv_heads * head_size].reshape(token_length, kv_heads, head_size)
    value_tensors = (
        kv_pre[:, kv_heads * head_size :]
        .reshape(token_length, kv_heads, head_size)
        .astype(jnp.bfloat16)
    )
    queries = head_prep(cosine, sine, query_pre, query_gain.astype(jnp.float32)).astype(
        jnp.bfloat16
    )
    key_tensors = head_prep(cosine, sine, key_pre, key_gain.astype(jnp.float32)).astype(
        jnp.bfloat16
    )
    select_low = selector.astype(jnp.bfloat16)
    keys_local = jnp.einsum(
        "hk,skd->shd", select_low, key_tensors, preferred_element_type=jnp.float32
    ).astype(jnp.bfloat16)
    values_local = jnp.einsum(
        "hk,skd->shd", select_low, value_tensors, preferred_element_type=jnp.float32
    ).astype(jnp.bfloat16)
    scores = attention_scores(queries, keys_local)
    highest = jnp.max(scores, axis=-1, keepdims=True)
    expos = jnp.exp(scores - highest)
    total_sums = jnp.sum(expos, axis=-1, keepdims=True)
    probs = expos / total_sums
    log_total = highest + jnp.log(total_sums)
    mixed = jnp.einsum(
        "hqk,khd->qhd", probs.astype(jnp.bfloat16), values_local, preferred_element_type=jnp.float32
    )
    mixed = mixed.astype(jnp.bfloat16).reshape(token_length, local_heads * head_size)
    middle = tokens + spread(forward_term(mixed, out_weight), row_count)
    normed_ffn = rms_scale(middle, ffn_norm.astype(jnp.float32)).astype(jnp.bfloat16)
    whole_ffn = collect(normed_ffn)
    gate = product(whole_ffn, gate_weight)
    upward = product(whole_ffn, up_weight)
    hidden = gated_product(gate, upward).astype(jnp.bfloat16)
    result = middle + spread(forward_term(hidden, down_weight), row_count)
    kept = (
        tokens,
        normed,
        whole,
        query_pre,
        key_pre,
        queries,
        keys_local,
        values_local,
        log_total,
        mixed,
        middle,
        whole_ffn,
        gate,
        upward,
        hidden,
    )
    return (result, kept)


def layer_backward(grad_rows, full, kept, query_gain, key_gain, tables, selector):
    (
        attn_norm,
        query_weight,
        key_value_weight,
        out_weight,
        ffn_norm,
        gate_weight,
        up_weight,
        down_weight,
    ) = full
    (
        tokens,
        normed,
        whole,
        query_pre,
        key_pre,
        queries,
        keys_local,
        values_local,
        log_total,
        mixed,
        middle,
        whole_ffn,
        gate,
        upward,
        hidden,
    ) = kept
    cosine, sine = tables
    head_size = query_gain.shape[0]
    local_heads = query_weight.shape[1] // head_size
    row_count = grad_rows.shape[0]
    token_length = whole.shape[0]
    grad_whole = collect(grad_rows)
    grad_hidden = right_transposed(grad_whole, down_weight)
    down_grad = left_transposed(hidden, grad_whole)
    _, silu_pull = jax.vjp(gated_product, gate, upward)
    grad_gate, grad_up = silu_pull(grad_hidden)
    grad_gate = grad_gate.astype(jnp.bfloat16)
    grad_up = grad_up.astype(jnp.bfloat16)
    gate_grad = left_transposed(whole_ffn, grad_gate)
    up_grad = left_transposed(whole_ffn, grad_up)

    def ffn_term(first_row, row_span):
        return right_transposed(grad_gate, gate_weight) + right_transposed(grad_up, up_weight)

    grad_normed_ffn = spread(ffn_term, row_count)
    _, ffn_pull = jax.vjp(rms_scale, middle, ffn_norm.astype(jnp.float32))
    grad_middle_part, ffn_norm_grad = ffn_pull(grad_normed_ffn)
    grad_middle = grad_rows.astype(jnp.float32) + grad_middle_part
    grad_attn = collect(grad_middle.astype(jnp.bfloat16))
    out_grad = left_transposed(mixed, grad_attn)
    grad_mixed = (
        right_transposed(grad_attn, out_weight)
        .astype(jnp.bfloat16)
        .reshape(token_length, local_heads, head_size)
    )
    scores = attention_scores(queries, keys_local)
    probs = jnp.exp(scores - log_total)
    grad_probs = jnp.einsum(
        "qhd,khd->hqk", grad_mixed, values_local, preferred_element_type=jnp.float32
    )
    grad_scores = probs * (grad_probs - jnp.sum(probs * grad_probs, axis=-1, keepdims=True))
    grad_scores = grad_scores.astype(jnp.bfloat16)
    scale_factor = head_size ** (-0.5)
    grad_queries = (
        jnp.einsum("hqk,khd->qhd", grad_scores, keys_local, preferred_element_type=jnp.float32)
        * scale_factor
    )
    grad_keys_local = (
        jnp.einsum("hqk,qhd->khd", grad_scores, queries, preferred_element_type=jnp.float32)
        * scale_factor
    )
    grad_values_local = jnp.einsum(
        "hqk,qhd->khd", probs.astype(jnp.bfloat16), grad_mixed, preferred_element_type=jnp.float32
    )
    select_wide = selector.astype(jnp.float32)
    grad_keys = jnp.einsum(
        "hk,shd->skd", select_wide, grad_keys_local, precision=lax.Precision.HIGHEST
    )
    grad_values = jnp.einsum(
        "hk,shd->skd", select_wide, grad_values_local, precision=lax.Precision.HIGHEST
    )
    _, query_pull = jax.vjp(
        partial(head_prep, cosine, sine), query_pre, query_gain.astype(jnp.float32)
    )
    grad_query_pre, query_gain_grad = query_pull(grad_queries)
    grad_query_pre = grad_query_pre.reshape(token_length, -1).astype(jnp.bfloat16)
    _, key_pull = jax.vjp(partial(head_prep, cosine, sine), key_pre, key_gain.astype(jnp.float32))
    grad_key_pre, key_gain_grad = key_pull(grad_keys)
    key_rows, value_rows = (
        lax.psum_scatter(
            grad_key_pre.reshape(token_length, -1).astype(jnp.bfloat16),
            "tensor",
            scatter_dimension=0,
            tiled=True,
        ).astype(jnp.float32),
        lax.psum_scatter(
            grad_values.reshape(token_length, -1).astype(jnp.bfloat16),
            "tensor",
            scatter_dimension=0,
            tiled=True,
        ).astype(jnp.float32),
    )
    grad_kv = jnp.concatenate([key_rows, value_rows], axis=1).astype(jnp.bfloat16)
    query_grad = left_transposed(whole, grad_query_pre)
    kv_grad = left_transposed(normed, grad_kv)

    def query_term(first_row, row_span):
        return right_transposed(grad_query_pre, query_weight)

    grad_normed = spread(query_term, row_count) + right_transposed(grad_kv, key_value_weight)
    _, input_pull = jax.vjp(rms_scale, tokens, attn_norm.astype(jnp.float32))
    grad_tokens_part, attn_norm_grad = input_pull(grad_normed)
    grad_tokens = grad_middle + grad_tokens_part
    return (
        grad_tokens,
        (
            attn_norm_grad,
            query_grad,
            kv_grad,
            out_grad,
            ffn_norm_grad,
            gate_grad,
            up_grad,
            down_grad,
            query_gain_grad,
            key_gain_grad,
        ),
    )


def local(
    inputs,
    attn_norm,
    query_weight,
    key_value_weight,
    out_weight,
    ffn_norm,
    gate_weight,
    up_weight,
    down_weight,
    query_gain,
    key_gain,
    cotangent,
):
    shard_count = lax.axis_size("dp")
    token_length = inputs.shape[1] * lax.axis_size("tensor")
    head_size = query_gain.shape[0]
    tables = rope_tables(token_length, head_size)
    selector = head_select(
        query_weight.shape[1] // head_size, key_value_weight.shape[1] // (2 * head_size)
    )
    total_sums = (
        jnp.zeros((attn_norm.shape[0] * shard_count,), jnp.float32),
        jnp.zeros((query_weight.shape[0] * shard_count, query_weight.shape[1]), jnp.float32),
        jnp.zeros(
            (key_value_weight.shape[0] * shard_count, key_value_weight.shape[1]), jnp.float32
        ),
        jnp.zeros((out_weight.shape[0], out_weight.shape[1] * shard_count), jnp.float32),
        jnp.zeros((ffn_norm.shape[0] * shard_count,), jnp.float32),
        jnp.zeros((gate_weight.shape[0] * shard_count, gate_weight.shape[1]), jnp.float32),
        jnp.zeros((up_weight.shape[0] * shard_count, up_weight.shape[1]), jnp.float32),
        jnp.zeros((down_weight.shape[0], down_weight.shape[1] * shard_count), jnp.float32),
    )
    gain_totals = (jnp.zeros((head_size,), jnp.float32), jnp.zeros((head_size,), jnp.float32))
    results = []
    input_grads = []
    for micro_index in range(inputs.shape[0]):
        full = fetch(
            attn_norm,
            query_weight,
            key_value_weight,
            out_weight,
            ffn_norm,
            gate_weight,
            up_weight,
            down_weight,
        )
        result, kept = layer_forward(
            inputs[micro_index], full, query_gain, key_gain, tables, selector
        )
        full = fetch(
            attn_norm,
            query_weight,
            key_value_weight,
            out_weight,
            ffn_norm,
            gate_weight,
            up_weight,
            down_weight,
        )
        grad_tokens, gradient_list = layer_backward(
            cotangent[micro_index], full, kept, query_gain, key_gain, tables, selector
        )
        added_terms = gradient_list[:8]
        total_sums = tuple(
            (
                running_total + added_term
                for running_total, added_term in zip(total_sums, added_terms)
            )
        )
        gain_totals = (gain_totals[0] + gradient_list[8], gain_totals[1] + gradient_list[9])
        results.append(result.astype(jnp.bfloat16))
        input_grads.append(grad_tokens)
    reduced = (
        lax.psum_scatter(total_sums[0], "dp", scatter_dimension=0, tiled=True),
        lax.psum_scatter(total_sums[1], "dp", scatter_dimension=0, tiled=True),
        lax.psum_scatter(total_sums[2], "dp", scatter_dimension=0, tiled=True),
        lax.psum_scatter(total_sums[3], "dp", scatter_dimension=1, tiled=True),
        lax.psum_scatter(total_sums[4], "dp", scatter_dimension=0, tiled=True),
        lax.psum_scatter(total_sums[5], "dp", scatter_dimension=0, tiled=True),
        lax.psum_scatter(total_sums[6], "dp", scatter_dimension=0, tiled=True),
        lax.psum_scatter(total_sums[7], "dp", scatter_dimension=1, tiled=True),
    )
    attn_norm_grad, kv_weight_grad, ffn_norm_grad = (
        lax.psum(reduced[0].astype(jnp.bfloat16), "tensor").astype(jnp.float32),
        lax.psum(reduced[2].astype(jnp.bfloat16), "tensor").astype(jnp.float32),
        lax.psum(reduced[4].astype(jnp.bfloat16), "tensor").astype(jnp.float32),
    )
    query_gain_grad, key_gain_grad = lax.psum((gain_totals[0], gain_totals[1]), ("dp", "tensor"))
    return (
        jnp.stack(results),
        jnp.stack(input_grads),
        attn_norm_grad,
        reduced[1],
        kv_weight_grad,
        reduced[3],
        ffn_norm_grad,
        reduced[5],
        reduced[6],
        reduced[7],
        query_gain_grad,
        key_gain_grad,
    )


def solution(mesh):
    placed = (
        P("dp", "tensor", None),
        P("dp"),
        P("dp", "tensor"),
        P("dp", None),
        P("tensor", "dp"),
        P("dp"),
        P("dp", "tensor"),
        P("dp", "tensor"),
        P("tensor", "dp"),
        P(),
        P(),
        P("dp", "tensor", None),
    )
    return jax.shard_map(
        local,
        mesh=mesh,
        in_specs=placed,
        out_specs=(
            P("dp", "tensor", None),
            P("dp", "tensor", None),
            P("dp"),
            P("dp", "tensor"),
            P("dp", None),
            P("tensor", "dp"),
            P("dp"),
            P("dp", "tensor"),
            P("dp", "tensor"),
            P("tensor", "dp"),
            P(),
            P(),
        ),
        check_vma=False,
    )
```

profile of v0, /device:TPU:0, one launch (start us, length us, event | category | flops | bytes accessed | tf_op | source)
XLA Modules:
  0.0 1463.0 jit_solution(8078153759097914511)
XLA Ops:
  9.7 22.2 %all-gather.2 = bf16[8,1,256]{2,1,0:T(2,128)(2,1)S(1)} all-gather(bf16[1,1,256]{2,1,0:T(2,128)(2,1)S(1)} %reshape.316), channel_id=1, replica_groups=mesh['dp'=8,'tensor'=4] {'dp'}, dimensions={0}, use_global_device_ids=true | all-gather | bytes 4608 | tf_op jit(solution)/shard_map/all_gather | solution.py:83
  32.0 2.0 fusion.45
  39.0 9.2 all-gather.35.cloned.1.call-done
  48.2 44.3 %all-gather.23.cloned.1.call-done = bf16[2048,320]{0,1:T(8,128)(2,1)} async-done(((bf16[256,320]{0,1:T(8,128)(2,1)}), bf16[2048,320]{0,1:T(8,128)(2,1)}) %all-gather.23.cloned.1.call-update) | async-done | bytes 1310736 | tf_op jit(solution)/shard_map/all_gather | solution.py:84
  92.6 2.3 fusion.145
  94.9 14.6 all-gather.19.cloned.1.call-done
  113.6 52.7 %all-gather.21.cloned.1.call-done = bf16[2048,640]{1,0:T(8,128)(2,1)} async-done(((bf16[256,640]{1,0:T(8,128)(2,1)}), bf16[2048,640]{1,0:T(8,128)(2,1)}) %all-gather.21.cloned.1.call-update) | async-done | bytes 2621456 | tf_op jit(solution)/shard_map/all_gather | solution.py:85
  166.3 3.2 fusion.144
  170.6 2.2 fusion.140
  179.5 29.5 %all-gather.25.cloned.1.call-done = bf16[320,2048]{1,0:T(8,128)(2,1)} async-done(((bf16[320,256]{1,0:T(8,128)(2,1)}), bf16[320,2048]{1,0:T(8,128)(2,1)}) %all-gather.25.cloned.1.call-update) | async-done | bytes 1310736 | tf_op jit(solution)/shard_map/all_gather | solution.py:86
  209.0 3.1 convolution_convert_fusion.4
  219.7 18.2 %all-gather.3 = bf16[8,1,256]{2,1,0:T(2,128)(2,1)S(1)} all-gather(bf16[1,1,256]{2,1,0:T(2,128)(2,1)S(1)} %reshape.318), channel_id=1, replica_groups=mesh['dp'=8,'tensor'=4] {'dp'}, dimensions={0}, use_global_device_ids=true | all-gather | bytes 4608 | tf_op jit(solution)/shard_map/all_gather | solution.py:87
  237.9 26.1 %reduce-scatter.27.cloned.1.call-done = bf16[64,2048]{1,0:T(8,128)(2,1)} async-done(((bf16[256,2048]{1,0:T(8,128)(2,1)}), bf16[64,2048]{1,0:T(8,128)(2,1)}) %reduce-scatter.27.cloned.1.call-update) | async-done | bytes 262160 | tf_op jit(solution)/shard_map/reduce_scatter | solution.py:64
  266.4 2.0 multiply_convert_fusion.7
  273.1 53.0 %all-gather.31.cloned.1.call-done = bf16[2048,704]{0,1:T(8,128)(2,1)} async-done(((bf16[256,704]{0,1:T(8,128)(2,1)}), bf16[2048,704]{0,1:T(8,128)(2,1)}) %all-gather.31.cloned.1.call-update) | async-done | bytes 2883600 | tf_op jit(solution)/shard_map/all_gather | solution.py:89
  326.2 17.1 %all-gather.37.cloned.1.call-done = bf16[256,2048]{1,0:T(8,128)(2,1)} async-done(((bf16[64,2048]{1,0:T(8,128)(2,1)}), bf16[256,2048]{1,0:T(8,128)(2,1)}) %all-gather.37.cloned.1.call-update) | async-done | bytes 1048592 | tf_op jit(solution)/shard_map/all_gather | solution.py:60
  343.2 4.0 fusion.147
  347.2 58.0 %all-gather.29.cloned.1.call-done = bf16[2048,704]{0,1:T(8,128)(2,1)} async-done(((bf16[256,704]{0,1:T(8,128)(2,1)}), bf16[2048,704]{0,1:T(8,128)(2,1)}) %all-gather.29.cloned.1.call-update) | async-done | bytes 2883600 | tf_op jit(solution)/shard_map/all_gather | solution.py:88
  405.2 4.0 fusion.146
  409.1 13.1 all-gather.45.cloned.1.call-done
  422.3 61.9 %all-gather.33.cloned.1.call-done = bf16[704,2048]{1,0:T(8,128)(2,1)} async-done(((bf16[704,256]{1,0:T(8,128)(2,1)}), bf16[704,2048]{1,0:T(8,128)(2,1)}) %all-gather.33.cloned.1.call-update) | async-done | bytes 2883600 | tf_op jit(solution)/shard_map/all_gather | solution.py:90
  484.2 4.5 multiply_convert_fusion.2
  490.9 2.0 fusion.1
  493.0 8.3 all-gather.27.cloned.1.call-done
  501.3 4.1 fusion.143
  507.2 12.8 all-gather.43.cloned.1.call-done
  520.1 4.5 multiply_convert_fusion.3
  526.7 2.0 fusion
  528.7 4.2 convolution_convert_fusion
  533.0 14.4 reduce-scatter.39.cloned.1.call-done
  547.4 28.1 %reduce-scatter.35.cloned.1.call-done = bf16[64,2048]{1,0:T(8,128)(2,1)} async-done(((bf16[256,2048]{1,0:T(8,128)(2,1)}), bf16[64,2048]{1,0:T(8,128)(2,1)}) %reduce-scatter.35.cloned.1.call-update) | async-done | bytes 262160 | tf_op jit(solution)/shard_map/reduce_scatter | solution.py:64
  575.4 2.2 fusion.49
  580.1 22.7 %reduce-scatter.33.cloned.1.call-done = bf16[64,2048]{1,0:T(8,128)(2,1)} async-done(((bf16[256,2048]{1,0:T(8,128)(2,1)}), bf16[64,2048]{1,0:T(8,128)(2,1)}) %reduce-scatter.33.cloned.1.call-update) | async-done | bytes 262160 | tf_op jit(solution)/shard_map/reduce_scatter | solution.py:64
  602.7 2.7 fusion.130
  607.9 14.4 all-gather.39.cloned.1.call-done
  622.3 2.2 convolution_convert_fusion.13
  625.7 2.1 multiply_reduce_fusion.1
  627.7 13.6 all-gather.41.cloned.1.call-done
  641.3 2.2 convolution_convert_fusion.12
  643.9 2.1 multiply_reduce_fusion
  653.4 1.9 multiply_reduce_fusion.5
  659.9 9.0 reduce-scatter.61.cloned.1.call-done
  669.8 22.0 %reduce-scatter.57.cloned.1.call-done = bf16[64,320]{1,0:T(8,128)(2,1)} async-done(((bf16[256,320]{1,0:T(8,128)(2,1)}), bf16[64,320]{1,0:T(8,128)(2,1)}) %reduce-scatter.57.cloned.1.call-update) | async-done | bytes 40976
  692.7 22.0 %reduce-scatter.55.cloned.1.call-done = bf16[64,320]{1,0:T(8,128)(2,1)} async-done(((bf16[256,320]{1,0:T(8,128)(2,1)}), bf16[64,320]{1,0:T(8,128)(2,1)}) %reduce-scatter.55.cloned.1.call-update) | async-done | bytes 40976
  715.7 3.3 fusion.87
  718.9 18.7 %reduce-scatter.59.cloned.1.call-done = bf16[64,320]{1,0:T(8,128)(2,1)} async-done(((bf16[256,320]{1,0:T(8,128)(2,1)}), bf16[64,320]{1,0:T(8,128)(2,1)}) %reduce-scatter.59.cloned.1.call-update) | async-done | bytes 40976
  738.6 5.8 convolution_add_fusion.3
  751.2 4.1 convolution_convert_fusion.1
  757.3 89.8 %reduce-scatter.45.cloned.1.call-done = f32[256,640]{1,0:T(8,128)} async-done(((f32[2048,640]{1,0:T(8,128)}), f32[256,640]{1,0:T(8,128)}) %reduce-scatter.45.cloned.1.call-update) | async-done | bytes 655376 | tf_op jit(solution)/shard_map/reduce_scatter | solution.py:404
  849.1 3.2 convolution_add_fusion.4
  854.2 2.1 convolution_add_fusion.5
  858.6 3.4 convolution_add_fusion.2
  864.3 3.5 convolution_add_fusion
  869.7 3.4 convolution_add_fusion.1
  875.1 40.2 %all-reduce.10 = (f32[64]{0:T(128)}, f32[64]{0:T(128)}) all-reduce(f32[64]{0:T(128)S(1)} %add.312, f32[64]{0:T(128)S(1)} %add.313), channel_id=1, replica_groups=mesh['dp'=8,'tensor'=4] {'dp','tensor'}, use_global_device_ids=true, to_apply=%region_51.52 | all-reduce | flops 128 | bytes 1024 | tf_op jit(solution)/shard_map/psum | solution.py:416
  915.3 2.7 convolution_add_fusion.8
  918.1 3.1 fusion.46
  921.3 36.8 %all-reduce.11 = (bf16[2048]{0:T(1024)(128)(2,1)S(1)}, bf16[2048]{0:T(1024)(128)(2,1)S(1)}) all-reduce(f32[2048]{0:T(1024)S(1)} %add.304, f32[2048]{0:T(1024)S(1)} %add.308), channel_id=16, replica_groups=mesh['dp'=8,'tensor'=4] {'dp'}, use_global_device_ids=true, to_apply=%region_36.37.clone | all-reduce | flops 4096 | bytes 24576
  958.2 6.0 all-reduce.12
  971.4 68.3 %reduce-scatter.43.cloned.1.call-done = f32[256,320]{0,1:T(8,128)} async-done(((f32[2048,320]{0,1:T(8,128)}), f32[256,320]{0,1:T(8,128)}) %reduce-scatter.43.cloned.1.call-update) | async-done | bytes 327696 | tf_op jit(solution)/shard_map/reduce_scatter | solution.py:403
  1039.6 73.8 %reduce-scatter.47.cloned.1.call-done = f32[320,256]{1,0:T(8,128)} async-done(((f32[320,2048]{1,0:T(8,128)}), f32[320,256]{1,0:T(8,128)}) %reduce-scatter.47.cloned.1.call-update) | async-done | bytes 327696 | tf_op jit(solution)/shard_map/reduce_scatter | solution.py:405
  1113.5 113.6 %reduce-scatter.53.cloned.1.call-done = f32[704,256]{1,0:T(8,128)} async-done(((f32[704,2048]{1,0:T(8,128)}), f32[704,256]{1,0:T(8,128)}) %reduce-scatter.53.cloned.1.call-update) | async-done | bytes 720912 | tf_op jit(solution)/shard_map/reduce_scatter | solution.py:409
  1227.0 114.4 %reduce-scatter.51.cloned.1.call-done = f32[256,704]{0,1:T(8,128)} async-done(((f32[2048,704]{0,1:T(8,128)}), f32[256,704]{0,1:T(8,128)}) %reduce-scatter.51.cloned.1.call-update) | async-done | bytes 720912 | tf_op jit(solution)/shard_map/reduce_scatter | solution.py:408
  1341.4 114.3 %reduce-scatter.49.cloned.1.call-done = f32[256,704]{0,1:T(8,128)} async-done(((f32[2048,704]{0,1:T(8,128)}), f32[256,704]{0,1:T(8,128)}) %reduce-scatter.49.cloned.1.call-update) | async-done | bytes 720912 | tf_op jit(solution)/shard_map/reduce_scatter | solution.py:407
  (471 shorter events, 88.1 us)
Async XLA Ops:
  7.2 30.2 %copy-start.137 = (bf16[64]{0:T(256)(128)(2,1)S(1)}, bf16[64]{0:T(256)(128)(2,1)}, u32[]{:S(2)}) copy-start(bf16[64]{0:T(256)(128)(2,1)} %param.21) | copy-start | bytes 388
  7.2 30.3 %copy-start.138 = (bf16[64]{0:T(256)(128)(2,1)S(1)}, bf16[64]{0:T(256)(128)(2,1)}, u32[]{:S(2)}) copy-start(bf16[64]{0:T(256)(128)(2,1)} %param.22) | copy-start | bytes 388
  7.2 41.0 %all-gather.35.cloned.1.call-start = ((), (), s32[]{:S(2)}) async-start(), calls=%async_computation.28 | async-start | bytes 1310720 | tf_op jit(solution)/shard_map/all_gather | solution.py:60
  9.2 28.3 %copy-start.123 = (f32[64]{0:T(128)}, f32[64]{0:T(128)S(1)}, u32[]{:S(2)}) copy-start(f32[64]{0:T(128)S(1)} %fusion.121) | copy-start | bytes 772
  9.7 27.7 %copy-start.121 = (f32[64]{0:T(128)}, f32[64]{0:T(128)S(1)}, u32[]{:S(2)}) copy-start(f32[64]{0:T(128)S(1)} %fusion.123) | copy-start | bytes 772
  34.0 58.5 %all-gather.23.cloned.1.call-start = ((), (), s32[]{:S(2)}) async-start(), calls=%async_computation.20 | async-start | bytes 1474560 | tf_op jit(solution)/shard_map/all_gather | solution.py:84
  34.8 74.8 %all-gather.19.cloned.1.call-start = ((), (), s32[]{:S(2)}) async-start(), calls=%async_computation.18 | async-start | bytes 1310720 | tf_op jit(solution)/shard_map/all_gather | solution.py:60
  35.5 130.7 %all-gather.21.cloned.1.call-start = ((), (), s32[]{:S(2)}) async-start(), calls=%async_computation.19 | async-start | bytes 2949120 | tf_op jit(solution)/shard_map/all_gather | solution.py:85
  36.1 172.9 %all-gather.25.cloned.1.call-start = ((), (), s32[]{:S(2)}) async-start(), calls=%async_computation.21 | async-start | bytes 1474560 | tf_op jit(solution)/shard_map/all_gather | solution.py:86
  36.7 201.2 %reduce-scatter.31.cloned.1.call-start = ((), (), s32[]{:S(2)}) async-start(), calls=%async_computation.29 | async-start | bytes 1310720 | tf_op jit(solution)/shard_map/reduce_scatter | solution.py:64
  37.4 140.1 %copy-start.109 = (s32[5]{0:T(128)}, s32[5]{0:T(128)S(1)}, u32[]{:S(2)}) copy-start(s32[5]{0:T(128)S(1)} %and_select_fusion) | copy-start | bytes 64
  37.5 73.9 %copy-start.119 = (f32[64]{0:T(128)}, f32[64]{0:T(128)S(1)}, u32[]{:S(2)}) copy-start(f32[64]{0:T(128)S(1)} %convert_element_type.289) | copy-start | bytes 772
  37.5 138.0 %copy-start.117 = (f32[64]{0:T(128)}, f32[64]{0:T(128)S(1)}, u32[]{:S(2)}) copy-start(f32[64]{0:T(128)S(1)} %convert_element_type.291) | copy-start | bytes 772
  111.4 54.9 %copy-start.97 = (f32[256,5]{0,1:T(8,128)}, f32[256,5]{0,1:T(8,128)S(1)}, u32[]{:S(2)}) copy-start(f32[256,5]{0,1:T(8,128)S(1)} %multiply_reduce_fusion.15) | copy-start | bytes 15364
  111.4 54.9 %copy-start.89 = (f32[256,5]{0,1:T(8,128)}, f32[256,5]{0,1:T(8,128)S(1)}, u32[]{:S(2)}) copy-start(f32[256,5]{0,1:T(8,128)S(1)} %fusion.100) | copy-start | bytes 15364
  179.5 34.6 %copy-start.69 = (bf16[5,64,256]{2,1,0:T(8,128)(2,1)}, bf16[5,64,256]{2,1,0:T(8,128)(2,1)S(1)}, u32[]{:S(2)}) copy-start(bf16[5,64,256]{2,1,0:T(8,128)(2,1)S(1)} %convolution_convert_fusion.14) | copy-start | bytes 491524
  212.1 51.9 %reduce-scatter.27.cloned.1.call-start = ((), (), s32[]{:S(2)}) async-start(), calls=%async_computation.22 | async-start | bytes 1310720 | tf_op jit(solution)/shard_map/reduce_scatter | solution.py:64
  216.4 47.7 %copy-start = (bf16[2,64,2048]{2,1,0:T(8,128)(2,1)S(1)}, bf16[2,64,2048]{2,1,0:T(8,128)(2,1)}, u32[]{:S(2)}) copy-start(bf16[2,64,2048]{2,1,0:T(8,128)(2,1)} %param.12) | copy-start | bytes 1572868
  218.8 107.3 %all-gather.31.cloned.1.call-start = ((), (), s32[]{:S(2)}) async-start(), calls=%async_computation.25 | async-start | bytes 3244032 | tf_op jit(solution)/shard_map/all_gather | solution.py:89
  219.6 123.7 %all-gather.37.cloned.1.call-start = ((), (), s32[]{:S(2)}) async-start(), calls=%async_computation.30 | async-start | bytes 1310720 | tf_op jit(solution)/shard_map/all_gather | solution.py:60
  237.9 364.8 %copy-start.81 = (f32[8,1,256]{2,1,0:T(1,128)}, f32[8,1,256]{2,1,0:T(1,128)S(1)}, u32[]{:S(2)}) copy-start(f32[8,1,256]{2,1,0:T(1,128)S(1)} %convert_element_type.373) | copy-start | bytes 24580
  268.5 136.7 %all-gather.29.cloned.1.call-start = ((), (), s32[]{:S(2)}) async-start(), calls=%async_computation.24 | async-start | bytes 3244032 | tf_op jit(solution)/shard_map/all_gather | solution.py:88
  269.1 153.2 %all-gather.45.cloned.1.call-start = ((), (), s32[]{:S(2)}) async-start(), calls=%async_computation.46 | async-start | bytes 1310720 | tf_op jit(solution)/shard_map/all_gather | solution.py:60
  271.0 213.2 %all-gather.33.cloned.1.call-start = ((), (), s32[]{:S(2)}) async-start(), calls=%async_computation.26 | async-start | bytes 3244032 | tf_op jit(solution)/shard_map/all_gather | solution.py:90
  271.6 229.7 %all-gather.27.cloned.1.call-start = ((), (), s32[]{:S(2)}) async-start(), calls=%async_computation.23 | async-start | bytes 1310720 | tf_op jit(solution)/shard_map/all_gather | solution.py:60
  272.3 247.7 %all-gather.43.cloned.1.call-start = ((), (), s32[]{:S(2)}) async-start(), calls=%async_computation.45 | async-start | bytes 1310720 | tf_op jit(solution)/shard_map/all_gather | solution.py:60
  272.9 274.4 %reduce-scatter.39.cloned.1.call-start = ((), (), s32[]{:S(2)}) async-start(), calls=%async_computation.35 | async-start | bytes 1310720 | tf_op jit(solution)/shard_map/reduce_scatter | solution.py:64
  492.9 82.5 %reduce-scatter.35.cloned.1.call-start = ((), (), s32[]{:S(2)}) async-start(), calls=%async_computation.32 | async-start | bytes 1310720 | tf_op jit(solution)/shard_map/reduce_scatter | solution.py:64
  528.7 74.0 %reduce-scatter.33.cloned.1.call-start = ((), (), s32[]{:S(2)}) async-start(), calls=%async_computation.31 | async-start | bytes 1310720 | tf_op jit(solution)/shard_map/reduce_scatter | solution.py:64
  532.9 89.4 %all-gather.39.cloned.1.call-start = ((), (), s32[]{:S(2)}) async-start(), calls=%async_computation.33 | async-start | bytes 1310720 | tf_op jit(solution)/shard_map/all_gather | solution.py:60
  605.5 35.9 %all-gather.41.cloned.1.call-start = ((), (), s32[]{:S(2)}) async-start(), calls=%async_computation.36 | async-start | bytes 1310720 | tf_op jit(solution)/shard_map/all_gather | solution.py:60
  606.2 62.7 %reduce-scatter.61.cloned.1.call-start = ((), (), s32[]{:S(2)}) async-start(), calls=%async_computation.50 | async-start | bytes 245760
  649.0 42.8 %reduce-scatter.57.cloned.1.call-start = ((), (), s32[]{:S(2)}) async-start(), calls=%async_computation.48 | async-start | bytes 245760
  655.9 59.8 %copy-start.32 = (bf16[64,2048]{1,0:T(8,128)(2,1)S(1)}, bf16[64,2048]{1,0:T(8,128)(2,1)}, u32[]{:S(2)}) copy-start(bf16[64,2048]{1,0:T(8,128)(2,1)} %get-tuple-element.59) | copy-start | bytes 786436
  656.8 58.0 %reduce-scatter.55.cloned.1.call-start = ((), (), s32[]{:S(2)}) async-start(), calls=%async_computation.47 | async-start | bytes 245760
  659.0 78.7 %reduce-scatter.59.cloned.1.call-start = ((), (), s32[]{:S(2)}) async-start(), calls=%async_computation.49 | async-start | bytes 245760
  659.8 187.3 %reduce-scatter.45.cloned.1.call-start = ((), (), s32[]{:S(2)}) async-start(), calls=%async_computation.39 | async-start | bytes 5898240 | tf_op jit(solution)/shard_map/reduce_scatter | solution.py:404
  744.4 170.8 %reduce-scatter.41.cloned.1.call-start = ((), (), s32[]{:S(2)}) async-start(), calls=%async_computation.37 | async-start | bytes 1310720 | tf_op jit(solution)/shard_map/reduce_scatter | solution.py:64
  749.4 168.7 %reduce-scatter.37.cloned.1.call-start = ((), (), s32[]{:S(2)}) async-start(), calls=%async_computation.34 | async-start | bytes 1310720 | tf_op jit(solution)/shard_map/reduce_scatter | solution.py:64
  751.1 214.3 %reduce-scatter.29.cloned.1.call-start = ((), (), s32[]{:S(2)}) async-start(), calls=%async_computation.27 | async-start | bytes 1310720 | tf_op jit(solution)/shard_map/reduce_scatter | solution.py:64
  755.3 214.2 %all-reduce.15.cloned.1.call-start = ((), (), s32[]{:S(2)}) async-start(), calls=%async_computation.40 | async-start | bytes 655360 | tf_op jit(solution)/shard_map/psum | solution.py:413
  849.0 190.6 %reduce-scatter.43.cloned.1.call-start = ((), (), s32[]{:S(2)}) async-start(), calls=%async_computation.38 | async-start | bytes 2949120 | tf_op jit(solution)/shard_map/reduce_scatter | solution.py:403
  852.4 261.1 %reduce-scatter.47.cloned.1.call-start = ((), (), s32[]{:S(2)}) async-start(), calls=%async_computation.41 | async-start | bytes 2949120 | tf_op jit(solution)/shard_map/reduce_scatter | solution.py:405
  856.3 370.7 %reduce-scatter.53.cloned.1.call-start = ((), (), s32[]{:S(2)}) async-start(), calls=%async_computation.44 | async-start | bytes 6488064 | tf_op jit(solution)/shard_map/reduce_scatter | solution.py:409
  862.1 479.3 %reduce-scatter.51.cloned.1.call-start = ((), (), s32[]{:S(2)}) async-start(), calls=%async_computation.43 | async-start | bytes 6488064 | tf_op jit(solution)/shard_map/reduce_scatter | solution.py:408
  867.8 587.9 %reduce-scatter.49.cloned.1.call-start = ((), (), s32[]{:S(2)}) async-start(), calls=%async_computation.42 | async-start | bytes 6488064 | tf_op jit(solution)/shard_map/reduce_scatter | solution.py:407
  873.1 42.1 %copy-start.9 = (bf16[2048,640]{1,0:T(8,128)(2,1)S(1)}, bf16[2048,640]{1,0:T(8,128)(2,1)}, u32[]{:S(2)}) copy-start(bf16[2048,640]{1,0:T(8,128)(2,1)} %all-gather.21.cloned.1.call-done) | copy-start | bytes 7864324
  873.2 42.1 %copy-start.62 = (bf16[64,320]{0,1:T(8,128)(2,1)S(1)}, bf16[64,320]{0,1:T(8,128)(2,1)}, u32[]{:S(2)}) copy-start(bf16[64,320]{0,1:T(8,128)(2,1)} %copy-done.61) | copy-start | bytes 122884
  873.2 44.8 %copy-start.86 = (f32[8,1,256]{2,1,0:T(1,128)S(1)}, f32[8,1,256]{2,1,0:T(1,128)}, u32[]{:S(2)}) copy-start(f32[8,1,256]{2,1,0:T(1,128)} %copy-done.85) | copy-start | bytes 24580
  873.2 44.8 %copy-start.122 = (f32[64]{0:T(128)S(1)}, f32[64]{0:T(128)}, u32[]{:S(2)}) copy-start(f32[64]{0:T(128)} %copy-done.121) | copy-start | bytes 772
  873.2 44.8 %copy-start.124 = (f32[64]{0:T(128)S(1)}, f32[64]{0:T(128)}, u32[]{:S(2)}) copy-start(f32[64]{0:T(128)} %copy-done.123) | copy-start | bytes 772
  918.0 47.4 %copy-start.126 = (f32[64]{0:T(128)S(1)}, f32[64]{0:T(128)}, u32[]{:S(2)}) copy-start(f32[64]{0:T(128)} %copy-done.125) | copy-start | bytes 772
  918.0 47.4 %copy-start.128 = (f32[64]{0:T(128)S(1)}, f32[64]{0:T(128)}, u32[]{:S(2)}) copy-start(f32[64]{0:T(128)} %copy-done.127) | copy-start | bytes 772
  918.0 47.5 %copy-start.17 = (bf16[64,2048]{1,0:T(8,128)(2,1)S(1)}, bf16[64,2048]{1,0:T(8,128)(2,1)}, u32[]{:S(2)}) copy-start(bf16[64,2048]{1,0:T(8,128)(2,1)} %reduce-scatter.27.cloned.1.call-done) | copy-start | bytes 786436
  918.0 47.5 %copy-start.82 = (f32[8,1,256]{2,1,0:T(1,128)S(1)}, f32[8,1,256]{2,1,0:T(1,128)}, u32[]{:S(2)}) copy-start(f32[8,1,256]{2,1,0:T(1,128)} %copy-done.81) | copy-start | bytes 24580
  918.0 47.5 %copy-start.116 = (f32[64]{0:T(128)S(1)}, f32[64]{0:T(128)}, u32[]{:S(2)}) copy-start(f32[64]{0:T(128)} %copy-done.115) | copy-start | bytes 772
  918.0 47.5 %copy-start.130 = (f32[64]{0:T(128)S(1)}, f32[64]{0:T(128)}, u32[]{:S(2)}) copy-start(f32[64]{0:T(128)} %multiply_multiply_fusion.11) | copy-start | bytes 772
  921.2 46.0 %copy-start.58 = (bf16[1,64,2048]{2,1,0:T(8,128)(2,1)S(1)}, bf16[1,64,2048]{2,1,0:T(8,128)(2,1)}, u32[]{:S(2)}) copy-start(bf16[1,64,2048]{2,1,0:T(8,128)(2,1)} %get-tuple-element.54) | copy-start | bytes 786436
  921.2 46.9 %copy-start.16 = (bf16[64,2048]{1,0:T(8,128)(2,1)S(1)}, bf16[64,2048]{1,0:T(8,128)(2,1)}, u32[]{:S(2)}) copy-start(bf16[64,2048]{1,0:T(8,128)(2,1)} %reduce-scatter.31.cloned.1.call-done) | copy-start | bytes 786436
  921.2 46.8 %copy-start.22 = (bf16[2,64,2048]{2,1,0:T(8,128)(2,1)S(1)}, bf16[2,64,2048]{2,1,0:T(8,128)(2,1)}, u32[]{:S(2)}) copy-start(bf16[2,64,2048]{2,1,0:T(8,128)(2,1)} %param.23) | copy-start | bytes 1572868
  921.2 46.8 %copy-start.23 = (f32[64,2048]{1,0:T(8,128)S(1)}, f32[64,2048]{1,0:T(8,128)}, u32[]{:S(2)}) copy-start(f32[64,2048]{1,0:T(8,128)} %convolution_add_fusion.8) | copy-start | bytes 1572868
  921.2 46.8 %copy-start.33 = (bf16[64,2048]{1,0:T(8,128)(2,1)S(1)}, bf16[64,2048]{1,0:T(8,128)(2,1)}, u32[]{:S(2)}) copy-start(bf16[64,2048]{1,0:T(8,128)(2,1)} %reduce-scatter.39.cloned.1.call-done) | copy-start | bytes 786436
  921.2 46.8 %copy-start.114 = (f32[64]{0:T(128)S(1)}, f32[64]{0:T(128)}, u32[]{:S(2)}) copy-start(f32[64]{0:T(128)} %copy-done.113) | copy-start | bytes 772
  921.2 46.8 %copy-start.129 = (f32[64]{0:T(128)S(1)}, f32[64]{0:T(128)}, u32[]{:S(2)}) copy-start(f32[64]{0:T(128)} %multiply_multiply_fusion.9) | copy-start | bytes 772
  (110 other events, 322.8 us)
Sparse Core Ops, SparseCore 0:
  34.2 14.0 all-gather.34
  50.3 42.2 all-gather.22
  94.1 15.3 all-gather.18
  111.6 54.6 all-gather.20
  168.2 40.8 all-gather.24
  212.3 23.5 reduce-scatter.30
  239.1 24.8 reduce-scatter.26
  266.1 59.9 all-gather.30
  328.3 14.9 all-gather.36
  345.1 60.0 all-gather.28
  407.3 14.9 all-gather.44
  424.2 60.0 all-gather.32
  486.4 14.9 all-gather.26
  503.3 16.7 all-gather.42
  522.4 24.8 reduce-scatter.38
  550.5 24.8 reduce-scatter.34
  577.8 24.8 reduce-scatter.32
  605.6 16.7 all-gather.38
  624.6 16.7 all-gather.40
  649.1 19.7 reduce-scatter.60
  672.0 19.7 reduce-scatter.56
  695.0 19.7 reduce-scatter.54
  717.9 19.7 reduce-scatter.58
  744.5 102.5 reduce-scatter.44
  850.4 24.6 reduce-scatter.40
  877.4 24.8 reduce-scatter.36
  904.9 24.9 reduce-scatter.28
  932.3 32.3 all-reduce.14
  968.7 70.8 reduce-scatter.42
  1043.6 69.8 reduce-scatter.46
  1117.7 109.2 reduce-scatter.52
  1231.2 110.1 reduce-scatter.50
  1345.5 110.1 reduce-scatter.48
where the time goes:
time: 1470 us; the launch traced here: 1460 us
  waiting for transfers between devices  1150 us (78%)
  blocking collectives  123 us (8%)
  matrix products  106 us (7%)
  other arithmetic  37 us (3%)
  local copies, waits for them, and re-layouts  30.5 us (2%)
  between operations  17.5 us (1%)
    reduce_scatter x1, waiting for transfers between devices, local(): lax.psum_scatter(total_sums[6], 'dp', scatter_dimension=0, tiled=True)  114 us
    reduce_scatter x1, waiting for transfers between devices, local(): lax.psum_scatter(total_sums[5], 'dp', scatter_dimension=0, tiled=True)  114 us
    reduce_scatter x1, waiting for transfers between devices, local(): lax.psum_scatter(total_sums[7], 'dp', scatter_dimension=1, tiled=True)  114 us
    all_gather x8, waiting for transfers between devices, collect(): return lax.all_gather(rows_low, 'tensor', axis=0, tiled=True)  103 us
    reduce_scatter x8, waiting for transfers between devices, spread(): lax.psum_scatter(partial_term(jnp.int32(0), row_count * lax.axis_size('te...  91.3 us
    reduce_scatter x1, waiting for transfers between devices, local(): lax.psum_scatter(total_sums[2], 'dp', scatter_dimension=0, tiled=True)  89.8 us
    unnamed x37, waiting for transfers between devices  78.2 us
    reduce_scatter x1, waiting for transfers between devices, local(): lax.psum_scatter(total_sums[3], 'dp', scatter_dimension=1, tiled=True)  73.8 us
  transfers between devices with their start and end apart: 33, of which 28 were waited for; matrix products, arithmetic and copies ran while one was open for 9% of the time, Pallas kernels for 0%

commit v1 on v0

v1 whole, which is shorter than its diff:
```python
from functools import partial

import jax
import jax.numpy as jnp
import numpy as np
from jax import lax
from jax.sharding import PartitionSpec as P

norm_eps = 1e-06
rope_base = 10000.0
masked_score = -1e30
f32 = jnp.float32
bf16 = jnp.bfloat16

RING = (0, 2, 4, 6, 7, 5, 3, 1)
OFFSETS = (0, -1, 1, -2, 2, -3, 3, 4)
PLACE = {ring: slot for slot, ring in enumerate(OFFSETS)}


def nn(left, right):
    return lax.dot_general(left, right, (((1,), (0,)), ((), ())), preferred_element_type=f32)


def nt(left, right):
    return lax.dot_general(left, right, (((1,), (1,)), ((), ())), preferred_element_type=f32)


def tn(left, right):
    return lax.dot_general(left, right, (((0,), (0,)), ((), ())), preferred_element_type=f32)


def ringed():
    return lax.axis_size("dp") == len(RING)


def owner_tables():
    size = len(RING)
    owners = np.zeros((size, size), np.int32)
    inverse = np.zeros((size, size), np.int32)
    for index in range(size):
        spot = RING.index(index)
        for slot, offset in enumerate(OFFSETS):
            owner = RING[(spot + offset) % size]
            owners[index, slot] = owner
            inverse[index, owner] = slot
    return owners, inverse


def reorder(rows, table):
    size = table.shape[0]
    width = rows.shape[1] // size
    picks = jnp.asarray(table)[lax.axis_index("dp")]
    return jnp.concatenate(
        [lax.dynamic_slice_in_dim(rows, picks[i] * width, width, axis=1) for i in range(size)],
        axis=1,
    )


def to_ring(rows):
    return reorder(rows, owner_tables()[0]) if ringed() else rows


def from_ring(rows):
    return reorder(rows, owner_tables()[1]) if ringed() else rows


def step(rows, forward):
    size = len(RING)
    move = 1 if forward else -1
    return lax.ppermute(
        rows, "dp", [(RING[i], RING[(i + move) % size]) for i in range(size)]
    )


def gather_weights(shard):
    if not ringed():
        return lax.all_gather(shard, "dp", axis=1, tiled=True)
    half = shard.shape[0] // 2
    parts = {0: shard}
    ahead = behind = shard
    for hop in (1, 2, 3):
        ahead = step(ahead, True)
        behind = step(behind, False)
        parts[-hop] = ahead
        parts[hop] = behind
    parts[4] = jnp.concatenate([step(ahead[:half], True), step(behind[half:], False)], axis=0)
    return jnp.concatenate([parts[offset] for offset in OFFSETS], axis=1)


def reduce_weights(grads):
    if not ringed():
        return lax.psum_scatter(
            grads.astype(bf16), "dp", scatter_dimension=1, tiled=True
        ).astype(f32)
    size = len(RING)
    width = grads.shape[1] // size
    half = grads.shape[0] // 2

    def part(offset):
        slot = PLACE[offset]
        return grads[:, slot * width : (slot + 1) * width]

    ahead = step(part(4)[:half].astype(bf16), True)
    behind = step(part(4)[half:].astype(bf16), False)
    ahead = jnp.concatenate([part(3)[:half] + ahead, part(3)[half:]], axis=0)
    behind = jnp.concatenate([part(-3)[:half], part(-3)[half:] + behind], axis=0)
    for hop in (2, 1, 0):
        ahead = step(ahead.astype(bf16), True)
        behind = step(behind.astype(bf16), False)
        if hop:
            ahead = part(hop) + ahead
            behind = part(-hop) + behind
    return part(0) + ahead + behind


def swap(rows, bit):
    count = lax.axis_size("tensor")
    return lax.ppermute(rows, "tensor", [(i, i ^ bit) for i in range(count)])


def collect(rows):
    core = swap(rows, 1)
    across = swap(rows, 2)
    return jnp.concatenate([rows, core, across, swap(across, 1)], axis=0)


def spread(partial_sums):
    count = partial_sums.shape[0] // 4
    low = partial_sums.astype(bf16)
    block = [low[i * count : (i + 1) * count] for i in range(4)]
    other = swap(jnp.concatenate([block[1], block[3]], axis=0), 1)
    kept = partial_sums[:count] + other[:count]
    sent = partial_sums[2 * count : 3 * count] + other[count:]
    return kept + swap(sent.astype(bf16), 2)


def turn(values):
    half = values.shape[-1] // 2
    return jnp.concatenate([-values[..., half:], values[..., :half]], axis=-1)


def turn_back(values):
    half = values.shape[-1] // 2
    return jnp.concatenate([values[..., half:], -values[..., :half]], axis=-1)


def head_prep(pre, gain, cosine, sine):
    scale = lax.rsqrt(jnp.mean(pre * pre, axis=-1, keepdims=True) + norm_eps)
    scaled = pre * scale * gain
    return scaled * cosine + turn(scaled) * sine, scale


def head_back(grad, pre, scale, gain, cosine, sine):
    grad = grad * cosine + turn_back(grad * sine)
    gain_grad = jnp.sum(grad * pre * scale, axis=(0, 1, 2))
    lifted = grad * gain
    back = scale * lifted - pre * (scale**3) * jnp.mean(lifted * pre, axis=-1, keepdims=True)
    return back, gain_grad


def local(
    inputs,
    attn_norm,
    query_weight,
    key_value_weight,
    out_weight,
    ffn_norm,
    gate_weight,
    up_weight,
    down_weight,
    query_gain,
    key_gain,
    cotangent,
):
    ranks = lax.axis_size("tensor")
    rank = lax.axis_index("tensor")
    seqs, span, width = inputs.shape
    head = query_gain.shape[0]
    heads = query_weight.shape[1] // head
    kv_heads = key_value_weight.shape[1] // (2 * head)
    group = heads * ranks // kv_heads
    kv_first = [(i * heads) // group for i in range(ranks)]
    kv_last = [(i * heads + heads - 1) // group for i in range(ranks)]
    kv_local = max(b - a for a, b in zip(kv_first, kv_last)) + 1
    kv_start = jnp.asarray(
        np.asarray([min(a, kv_heads - kv_local) for a in kv_first], np.int32)
    )[rank]
    kv_of = (rank * heads + jnp.arange(heads, dtype=jnp.int32)) // group - kv_start
    rows = seqs * span
    hidden_units = gate_weight.shape[1]
    q_cols = heads * head
    kv_cols = kv_local * head

    attn_gain = attn_norm.astype(f32)
    ffn_gain = ffn_norm.astype(f32)
    key_weight = lax.dynamic_slice_in_dim(key_value_weight, kv_start * head, kv_cols, axis=1)
    value_weight = lax.dynamic_slice_in_dim(
        key_value_weight, (kv_heads + kv_start) * head, kv_cols, axis=1
    )
    qkv_own = jnp.concatenate([query_weight.T, key_weight.T, value_weight.T], axis=0)
    qkv_shard = (qkv_own.astype(f32) * attn_gain[None]).astype(bf16)
    gate_shard = (gate_weight.T.astype(f32) * ffn_gain[None]).astype(bf16)
    up_shard = (up_weight.T.astype(f32) * ffn_gain[None]).astype(bf16)
    qkv_full = gather_weights(qkv_shard)
    out_full = gather_weights(out_weight)
    gate_full = gather_weights(gate_shard)
    up_full = gather_weights(up_shard)
    down_full = gather_weights(down_weight)

    tokens_low = to_ring(inputs.reshape(rows, width))
    cot_low = to_ring(cotangent.reshape(rows, width))
    tokens = tokens_low.astype(f32)
    whole = collect(tokens_low)
    cot_whole = collect(cot_low)

    block_of = rank ^ jnp.arange(ranks, dtype=jnp.int32)
    positions = (block_of[:, None] * span + jnp.arange(span, dtype=jnp.int32)[None]).reshape(-1)
    inverse = rope_base ** (-2.0 * jnp.arange(head // 2, dtype=f32) / head)
    angles = positions.astype(f32)[:, None] * inverse[None]
    cosine = jnp.concatenate([jnp.cos(angles)] * 2, axis=-1)
    sine = jnp.concatenate([jnp.sin(angles)] * 2, axis=-1)
    seq_len = ranks * span

    def by_head(flat, count):
        return (
            flat.reshape(ranks, seqs, span, count, head)
            .transpose(1, 3, 0, 2, 4)
            .reshape(seqs, count, seq_len, head)
        )

    def by_row(split):
        count = split.shape[1]
        return (
            split.reshape(seqs, count, ranks, span, head)
            .transpose(2, 0, 3, 1, 4)
            .reshape(ranks * rows, count * head)
        )

    wide = whole.astype(f32)
    row_scale = lax.rsqrt(jnp.mean(wide * wide, axis=-1, keepdims=True) + norm_eps)
    qkv = nt(whole, qkv_full) * row_scale
    query_pre = by_head(qkv[:, :q_cols], heads)
    key_pre = by_head(qkv[:, q_cols : q_cols + kv_cols], kv_local)
    values = by_head(qkv[:, q_cols + kv_cols :].astype(bf16), kv_local)
    q_gain = query_gain.astype(f32)
    k_gain = key_gain.astype(f32)
    queries, query_scale = head_prep(query_pre, q_gain, cosine, sine)
    queries = queries.astype(bf16)
    keys, key_scale = head_prep(key_pre, k_gain, cosine, sine)
    keys = keys.astype(bf16)

    picks = [kv_of[:, None] == i for i in range(kv_local)]

    def to_heads(per_kv):
        out = per_kv[:, :1]
        for i in range(1, kv_local):
            out = jnp.where(picks[i][None, :, :, None], per_kv[:, i : i + 1], out)
        return jnp.broadcast_to(out, (seqs, heads, seq_len, head))

    def to_kv(per_head):
        return jnp.stack(
            [
                jnp.sum(jnp.where(picks[i][None, :, :, None], per_head, 0.0), axis=1)
                for i in range(kv_local)
            ],
            axis=1,
        )

    keys_h = to_heads(keys)
    values_h = to_heads(values)
    scores = jnp.einsum("shqd,shkd->shqk", queries, keys_h, preferred_element_type=f32)
    scores = scores * head ** (-0.5)
    causal = positions[:, None] >= positions[None, :]
    scores = jnp.where(causal[None, None], scores, masked_score)
    expos = jnp.exp(scores - jnp.max(scores, axis=-1, keepdims=True))
    soft = expos / jnp.sum(expos, axis=-1, keepdims=True)
    probs = soft.astype(bf16)
    mixed = by_row(
        jnp.einsum("shqk,shkd->shqd", probs, values_h, preferred_element_type=f32).astype(bf16)
    )
    middle = tokens + spread(nn(mixed, out_full))
    mid_scale = lax.rsqrt(jnp.mean(middle * middle, axis=-1, keepdims=True) + norm_eps)
    ffn_whole = collect((middle * mid_scale).astype(bf16))

    gate = nt(ffn_whole, gate_full)
    upward = nt(ffn_whole, up_full)
    sig = jax.nn.sigmoid(gate)
    silu = gate * sig
    hidden = (silu * upward).astype(bf16)
    down_grad = reduce_weights(tn(hidden, cot_whole))
    result = (middle + spread(nn(hidden, down_full))).astype(bf16)

    grad_hidden = nt(cot_whole, down_full)
    grad_gate = (grad_hidden * upward * sig * (1.0 + gate * (1.0 - sig))).astype(bf16)
    grad_up = (grad_hidden * silu).astype(bf16)
    lifted = spread(nn(grad_gate, gate_full) + nn(grad_up, up_full))
    gate_grad = reduce_weights(tn(grad_gate, ffn_whole))
    up_grad = reduce_weights(tn(grad_up, ffn_whole))
    grad_middle = (
        cot_low.astype(f32)
        + mid_scale * lifted
        - middle * mid_scale**3 * jnp.mean(lifted * middle, axis=-1, keepdims=True)
    )
    grad_attn = collect(grad_middle.astype(bf16))
    out_grad = reduce_weights(tn(mixed, grad_attn))
    grad_mixed = by_head(nt(grad_attn, out_full).astype(bf16), heads)

    grad_probs = jnp.einsum("shqd,shkd->shqk", grad_mixed, values_h, preferred_element_type=f32)
    grad_scores = (
        soft * (grad_probs - jnp.sum(soft * grad_probs, axis=-1, keepdims=True))
    ).astype(bf16)
    factor = head ** (-0.5)
    grad_queries = (
        jnp.einsum("shqk,shkd->shqd", grad_scores, keys_h, preferred_element_type=f32) * factor
    )
    grad_keys = to_kv(
        jnp.einsum("shqk,shqd->shkd", grad_scores, queries, preferred_element_type=f32) * factor
    )
    grad_values = to_kv(
        jnp.einsum("shqk,shqd->shkd", probs, grad_mixed, preferred_element_type=f32)
    )
    grad_query_pre, query_gain_grad = head_back(
        grad_queries, query_pre, query_scale, q_gain, cosine, sine
    )
    grad_key_pre, key_gain_grad = head_back(
        grad_keys, key_pre, key_scale, k_gain, cosine, sine
    )
    grad_qkv = jnp.concatenate(
        [by_row(grad_query_pre), by_row(grad_key_pre), by_row(grad_values)], axis=1
    )
    grad_qkv = (grad_qkv * row_scale).astype(bf16)
    lifted_attn = spread(nn(grad_qkv, qkv_full))
    qkv_grad = reduce_weights(tn(grad_qkv, whole))
    own_scale = lax.rsqrt(jnp.mean(tokens * tokens, axis=-1, keepdims=True) + norm_eps)
    input_grad = grad_middle + lifted_attn - tokens * own_scale**2 * jnp.mean(
        lifted_attn * tokens, axis=-1, keepdims=True
    )

    attn_norm_grad = jnp.sum(qkv_grad * qkv_own.astype(f32), axis=0)
    ffn_norm_grad = jnp.sum(
        gate_grad * gate_weight.T.astype(f32) + up_grad * up_weight.T.astype(f32), axis=0
    )
    norms = jnp.stack([attn_norm_grad, ffn_norm_grad])
    norms = norms + swap(norms, 1)
    norms = norms + swap(norms, 2)
    gains = jnp.stack([query_gain_grad, key_gain_grad])
    gains = lax.psum(gains, ("dp", "tensor"))

    qkv_grad = qkv_grad * attn_gain[None]
    kv_sum = jnp.zeros((2, kv_heads * head, qkv_grad.shape[1]), f32)
    kv_own = qkv_grad[q_cols:].reshape(2, kv_cols, -1)
    kv_sum = lax.dynamic_update_slice(kv_sum, kv_own, (0, kv_start * head, 0))
    for bit in (1, 2):
        kv_sum = lax.reduce_precision(kv_sum, 8, 7)
        kv_sum = kv_sum + swap(kv_sum.astype(bf16), bit)

    return (
        from_ring(result).reshape(inputs.shape),
        from_ring(input_grad).reshape(inputs.shape),
        norms[0],
        qkv_grad[:q_cols].T,
        kv_sum.reshape(2 * kv_heads * head, -1).T,
        out_grad,
        norms[1],
        (gate_grad * ffn_gain[None]).T,
        (up_grad * ffn_gain[None]).T,
        down_grad,
        gains[0],
        gains[1],
    )


def solution(mesh):
    placed = (
        P("dp", "tensor", None),
        P("dp"),
        P("dp", "tensor"),
        P("dp", None),
        P("tensor", "dp"),
        P("dp"),
        P("dp", "tensor"),
        P("dp", "tensor"),
        P("tensor", "dp"),
        P(),
        P(),
        P("dp", "tensor", None),
    )
    return jax.shard_map(
        local,
        mesh=mesh,
        in_specs=placed,
        out_specs=(
            P("dp", "tensor", None),
            P("dp", "tensor", None),
            P("dp"),
            P("dp", "tensor"),
            P("dp", None),
            P("tensor", "dp"),
            P("dp"),
            P("dp", "tensor"),
            P("dp", "tensor"),
            P("tensor", "dp"),
            P(),
            P(),
        ),
        check_vma=False,
    )
```

time: 1470 us -> 473 us (0.32)
  waiting for transfers between devices: 1150 us -> 158 us
  starting transfers between devices: 1.97 us -> 98.5 us
  blocking collectives: 123 us -> 38.6 us
  matrix products: 106 us -> 43.8 us
  local copies, waits for them, and re-layouts: 30.5 us -> 73.6 us
    reduce_scatter x14 -> x0, waiting for transfers between devices: 665 us -> none  [the longest x1 114 us: local(): lax.psum_scatter(total_sums[6], 'dp', scatter_dimension=0, tiled=True)]
    all_gather x14 -> x0, waiting for transfers between devices: 403 us -> none  [the longest x8 103 us: collect(): return lax.all_gather(rows_low, 'tensor', axis=0, tiled=True)]
    ppermute x0 -> x104, waiting for transfers between devices: none -> 158 us  [the longest x80 125 us: step(): lax.ppermute(rows, 'dp', [(RING[i], RING[(i + move) % size]) for i in ran...]
    ppermute x0 -> x104, starting transfers between devices: none -> 98.5 us  [the longest x80 87.5 us: step(): lax.ppermute(rows, 'dp', [(RING[i], RING[(i + move) % size]) for i in ran...]
    unnamed x37 -> x0, waiting for transfers between devices: 78.2 us -> none
    dot_general x56 -> x20, matrix products: 106 us -> 40.2 us  [the longest x5 14.1 us: nn(): lax.dot_general(left, right, (((1,), (0,)), ((), ())), preferred_element_...]
    all_gather x2 -> x0, blocking collectives: 40.5 us -> none  [the longest x1 22.2 us: fetch(): lax.all_gather(attn_norm, 'dp', axis=0, tiled=True)]
    unnamed x1 -> x0, blocking collectives: 36.8 us -> none
  transfers between devices with their start and end apart: 33 -> 104, of which waited for: 28 -> 46; matrix products, arithmetic and copies ran while one was open for 9% -> 23% of each run, Pallas kernels for 0% -> 0%
where the time goes in v1:
time: 473 us; the launch traced here: 466 us
  waiting for transfers between devices  158 us (33%)
  starting transfers between devices  98.5 us (21%)
  local copies, waits for them, and re-layouts  73.6 us (16%)
  matrix products  43.8 us (9%)
  other arithmetic  40.2 us (8%)
  blocking collectives  38.6 us (8%)
  between operations  13.5 us (3%)
    ppermute x80, waiting for transfers between devices, step(): lax.ppermute(rows, 'dp', [(RING[i], RING[(i + move) % size]) for i in ran...  125 us
    ppermute x80, starting transfers between devices, step(): lax.ppermute(rows, 'dp', [(RING[i], RING[(i + move) % size]) for i in ran...  87.5 us
    unnamed x229, local copies, waits for them, and re-layouts  42.9 us
    psum x1, blocking collectives, local(): gains = lax.psum(gains, ('dp', 'tensor'))  38.6 us
    ppermute x24, waiting for transfers between devices, swap(): return lax.ppermute(rows, 'tensor', [(i, i ^ bit) for i in range(count)])  33.3 us
    dot_general x5, matrix products, nn(): lax.dot_general(left, right, (((1,), (0,)), ((), ())), preferred_element_...  14.1 us
    ppermute x24, starting transfers between devices, swap(): return lax.ppermute(rows, 'tensor', [(i, i ^ bit) for i in range(count)])  11 us
    dot_general x5, matrix products, tn(): lax.dot_general(left, right, (((0,), (0,)), ((), ())), preferred_element_...  10.1 us
  transfers between devices with their start and end apart: 104, of which 46 were waited for; matrix products, arithmetic and copies ran while one was open for 23% of the time, Pallas kernels for 0%

profile of v1, /device:TPU:0, one launch (start us, length us, event | category | flops | bytes accessed | tf_op | source)
XLA Modules:
  0.0 466.2 jit_solution(8925057002941586893)
XLA Ops:
  2.7 1.8 constant_dynamic-update-slice_fusion.14
  4.5 3.0 collective-permute-start.3
  7.5 2.0 collective-permute-start.11
  9.5 2.0 collective-permute-start.40
  42.4 2.3 constant_dynamic-update-slice_fusion.28
  53.8 2.0 collective-permute-start.1
  59.0 1.7 constant_dynamic-update-slice_fusion.13
  61.1 1.7 constant_dynamic-update-slice_fusion.12
  72.7 1.8 collective-permute-done.32
  78.4 3.0 collective-permute-done.15
  88.6 13.1 %collective-permute-done.8 = bf16[576,256]{1,0:T(8,128)(2,1)S(1)} collective-permute-done((bf16[576,256]{1,0:T(8,128)(2,1)S(1)}, bf16[576,256]{1,0:T(8,128)(2,1)S(1)}, u32[]{:S(2)}, u32[]{:S(2)}) %collective-permute-start.8) | collective-permute-done | bytes 294944 | tf_op jit(solution)/shard_map/ppermute | solution.py:70
  104.0 3.2 collective-permute-done.10
  120.8 2.1 reshape.479
  127.7 3.5 fusion.148
  131.3 2.1 convolution_convert_fusion
  135.1 2.7 fusion.151
  147.8 2.9 collective-permute-done.34
  154.1 4.3 collective-permute-done.26
  163.4 5.7 %collective-permute-done.45 = bf16[704,256]{1,0:T(8,128)(2,1)S(1)} collective-permute-done((bf16[704,256]{1,0:T(8,128)(2,1)}, bf16[704,256]{1,0:T(8,128)(2,1)S(1)}, u32[]{:S(2)}, u32[]{:S(2)}) %collective-permute-start.45) | collective-permute-done | bytes 360480 | tf_op jit(solution)/shard_map/ppermute | solution.py:70
  171.3 4.6 collective-permute-done.37
  179.3 6.0 %collective-permute-done.51 = bf16[128,2048]{1,0:T(8,128)(2,1)S(1)} collective-permute-done((bf16[128,2048]{1,0:T(8,128)(2,1)S(1)}, bf16[128,2048]{1,0:T(8,128)(2,1)S(1)}, u32[]{:S(2)}, u32[]{:S(2)}) %collective-permute-start.51) | collective-permute-done | bytes 524320 | tf_op jit(solution)/shard_map/ppermute | solution.py:118
  187.7 2.3 collective-permute-done.47
  193.6 2.5 collective-permute-done.38
  198.6 3.0 collective-permute-done.30
  202.7 1.7 fusion.75
  204.6 1.7 fusion.127
  206.3 3.5 multiply_convert_fusion.2
  209.8 1.8 fusion.160
  211.6 1.8 fusion.152
  214.1 1.8 fusion.153
  216.0 1.7 fusion.155
  220.2 3.0 fusion.156
  225.5 3.0 fusion.159
  233.0 3.1 collective-permute-done.96
  238.3 5.5 %collective-permute-done.77 = bf16[704,256]{1,0:T(8,128)(2,1)S(1)} collective-permute-done((bf16[704,256]{1,0:T(8,128)(2,1)S(1)}, bf16[704,256]{1,0:T(8,128)(2,1)S(1)}, u32[]{:S(2)}, u32[]{:S(2)}) %collective-permute-start.77) | collective-permute-done | bytes 360480 | tf_op jit(solution)/shard_map/ppermute | solution.py:70
  245.4 6.1 %collective-permute-done.69 = bf16[704,256]{1,0:T(8,128)(2,1)S(1)} collective-permute-done((bf16[704,256]{1,0:T(8,128)(2,1)S(1)}, bf16[704,256]{1,0:T(8,128)(2,1)S(1)}, u32[]{:S(2)}, u32[]{:S(2)}) %collective-permute-start.69) | collective-permute-done | bytes 360480 | tf_op jit(solution)/shard_map/ppermute | solution.py:70
  253.2 6.1 %collective-permute-done.97 = bf16[704,256]{1,0:T(8,128)(2,1)S(1)} collective-permute-done((bf16[704,256]{1,0:T(8,128)(2,1)S(1)}, bf16[704,256]{1,0:T(8,128)(2,1)S(1)}, u32[]{:S(2)}, u32[]{:S(2)}) %collective-permute-start.97) | collective-permute-done | bytes 360480 | tf_op jit(solution)/shard_map/ppermute | solution.py:70
  261.5 5.5 %collective-permute-done.78 = bf16[704,256]{1,0:T(8,128)(2,1)S(1)} collective-permute-done((bf16[704,256]{1,0:T(8,128)(2,1)S(1)}, bf16[704,256]{1,0:T(8,128)(2,1)S(1)}, u32[]{:S(2)}, u32[]{:S(2)}) %collective-permute-start.78) | collective-permute-done | bytes 360480 | tf_op jit(solution)/shard_map/ppermute | solution.py:70
  268.7 6.0 %collective-permute-done.70 = bf16[704,256]{1,0:T(8,128)(2,1)S(1)} collective-permute-done((bf16[704,256]{1,0:T(8,128)(2,1)S(1)}, bf16[704,256]{1,0:T(8,128)(2,1)S(1)}, u32[]{:S(2)}, u32[]{:S(2)}) %collective-permute-start.70) | collective-permute-done | bytes 360480 | tf_op jit(solution)/shard_map/ppermute | solution.py:70
  277.0 5.5 %collective-permute-done.98 = bf16[704,256]{1,0:T(8,128)(2,1)S(1)} collective-permute-done((bf16[704,256]{1,0:T(8,128)(2,1)S(1)}, bf16[704,256]{1,0:T(8,128)(2,1)S(1)}, u32[]{:S(2)}, u32[]{:S(2)}) %collective-permute-start.98) | collective-permute-done | bytes 360480 | tf_op jit(solution)/shard_map/ppermute | solution.py:70
  286.2 7.5 %collective-permute-done.74 = bf16[704,256]{1,0:T(8,128)(2,1)S(1)} collective-permute-done((bf16[704,256]{1,0:T(8,128)(2,1)S(1)}, bf16[704,256]{1,0:T(8,128)(2,1)S(1)}, u32[]{:S(2)}, u32[]{:S(2)}) %collective-permute-start.74) | collective-permute-done | bytes 360480 | tf_op jit(solution)/shard_map/ppermute | solution.py:70
  295.3 2.9 collective-permute-done.102
  299.2 9.3 %collective-permute-done.49 = bf16[128,2048]{1,0:T(8,128)(2,1)S(1)} collective-permute-done((bf16[128,2048]{1,0:T(8,128)(2,1)S(1)}, bf16[128,2048]{1,0:T(8,128)(2,1)S(1)}, u32[]{:S(2)}, u32[]{:S(2)}) %collective-permute-start.49) | collective-permute-done | bytes 524320 | tf_op jit(solution)/shard_map/ppermute | solution.py:118
  308.6 1.7 fusion.130
  312.2 7.3 %collective-permute-done.56 = bf16[128,2048]{1,0:T(8,128)(2,1)S(1)} collective-permute-done((bf16[128,2048]{1,0:T(8,128)(2,1)S(1)}, bf16[128,2048]{1,0:T(8,128)(2,1)S(1)}, u32[]{:S(2)}, u32[]{:S(2)}) %collective-permute-start.56) | collective-permute-done | bytes 524320 | tf_op jit(solution)/shard_map/ppermute | solution.py:118
  320.6 2.5 collective-permute-done.75
  323.1 2.0 multiply_bitcast_fusion
  328.6 2.5 multiply_reduce_fusion.1
  340.3 1.8 concatenate.172
  342.1 1.8 concatenate.171
  343.9 2.5 fusion.54
  353.1 5.9 %fusion.154 = (bf16[512,2048]{1,0:T(8,128)(2,1)S(1)}, f32[512,2048]{1,0:T(8,128)}) fusion(bf16[576,2048]{1,0:T(8,128)(2,1)} %copy-done.7, f32[512,128]{0,1:T(8,128)S(1)} %copy-done.17, f32[512,128]{0,1:T(8,128)} %reshape.492, f32[512,320]{0,1:T(8,128)S(1)} %reshape.491, f32[512]{0:T(512)S(1)} %copy-done.52), kind=kOutput, calls=%fused_computation.383 | convolution fusion | flops 1210187776 | bytes 9832448 | tf_op jit(solution)/shard_map/dot_general | solution.py:21
  370.3 2.0 collective-permute-done.60
  378.0 3.6 collective-permute-done.90
  382.2 3.3 collective-permute-done.61
  386.8 38.6 %psum.7 = f32[2,64]{1,0:T(2,128)S(1)} all-reduce(f32[2,64]{1,0:T(2,128)S(1)} %pad_maximum_fusion.28), channel_id=1, replica_groups=mesh['dp'=8,'tensor'=4] {'dp','tensor'}, use_global_device_ids=true, to_apply=%region_20.21 | all-reduce | flops 128 | bytes 1024 | tf_op jit(solution)/shard_map/psum | solution.py:347
  430.4 2.3 collective-permute-start.66
  434.8 1.7 fusion.81
  437.1 2.2 collective-permute-done.66
  441.9 1.8 collective-permute-start.59
  443.7 4.0 collective-permute-done.67
  450.2 1.7 collective-permute-start.85
  455.7 1.7 collective-permute-start.87
  457.5 7.3 %collective-permute-done.87 = bf16[2,320,256]{2,1,0:T(8,128)(2,1)S(1)} collective-permute-done((bf16[2,320,256]{2,1,0:T(8,128)(2,1)S(1)}, bf16[2,320,256]{2,1,0:T(8,128)(2,1)S(1)}, u32[]{:S(2)}, u32[]{:S(2)}) %collective-permute-start.87) | collective-permute-done | bytes 327712 | tf_op jit(solution)/shard_map/ppermute | solution.py:118
  (571 shorter events, 197.5 us)
Async XLA Ops:
  4.5 52.9 %collective-permute-start.3 = (bf16[576,256]{1,0:T(8,128)(2,1)}, bf16[576,256]{1,0:T(8,128)(2,1)}, u32[]{:S(2)}, u32[]{:S(2)}) collective-permute-start(bf16[576,256]{1,0:T(8,128)(2,1)} %get-tuple-element.71), channel_id=1, source_target_pairs={{0,8},{8,16},{16,24},{24,28},{28,20},{20,12},{12,4},{4,0},{1,9},{9... | collective-permute-start | bytes 884744 | tf_op jit(solution)/shard_map/ppermute | solution.py:70
  7.5 53.2 %collective-permute-start.4 = (bf16[576,256]{1,0:T(8,128)(2,1)}, bf16[576,256]{1,0:T(8,128)(2,1)}, u32[]{:S(2)}, u32[]{:S(2)}) collective-permute-start(bf16[576,256]{1,0:T(8,128)(2,1)} %get-tuple-element.71), channel_id=1, source_target_pairs={{0,4},{8,0},{16,8},{24,16},{28,24},{20,28},{12,20},{4,12},{1,5},{9... | collective-permute-start | bytes 884744 | tf_op jit(solution)/shard_map/ppermute | solution.py:70
  7.5 44.7 %collective-permute-start.11 = (bf16[320,256]{1,0:T(8,128)(2,1)}, bf16[320,256]{1,0:T(8,128)(2,1)}, u32[]{:S(2)}, u32[]{:S(2)}) collective-permute-start(bf16[320,256]{1,0:T(8,128)(2,1)} %param.21), channel_id=1, source_target_pairs={{0,8},{8,16},{16,24},{24,28},{28,20},{20,12},{12,4},{4,0},{1,9},{9... | collective-permute-start | bytes 491528 | tf_op jit(solution)/shard_map/ppermute | solution.py:70
  9.5 44.2 %collective-permute-start.12 = (bf16[320,256]{1,0:T(8,128)(2,1)}, bf16[320,256]{1,0:T(8,128)(2,1)}, u32[]{:S(2)}, u32[]{:S(2)}) collective-permute-start(bf16[320,256]{1,0:T(8,128)(2,1)} %param.21), channel_id=1, source_target_pairs={{0,4},{8,0},{16,8},{24,16},{28,24},{20,28},{12,20},{4,12},{1,5},{9... | collective-permute-start | bytes 491528 | tf_op jit(solution)/shard_map/ppermute | solution.py:70
  9.5 59.0 %collective-permute-start.40 = (bf16[704,256]{1,0:T(8,128)(2,1)}, bf16[704,256]{1,0:T(8,128)(2,1)}, u32[]{:S(2)}, u32[]{:S(2)}) collective-permute-start(bf16[704,256]{1,0:T(8,128)(2,1)} %param.25), channel_id=1, source_target_pairs={{0,8},{8,16},{16,24},{24,28},{28,20},{20,12},{12,4},{4,0},{1,9},{9... | collective-permute-start | bytes 1081352 | tf_op jit(solution)/shard_map/ppermute | solution.py:70
  52.2 18.9 %collective-permute-start.41 = (bf16[704,256]{1,0:T(8,128)(2,1)}, bf16[704,256]{1,0:T(8,128)(2,1)}, u32[]{:S(2)}, u32[]{:S(2)}) collective-permute-start(bf16[704,256]{1,0:T(8,128)(2,1)} %param.25), channel_id=1, source_target_pairs={{0,4},{8,0},{16,8},{24,16},{28,24},{20,28},{12,20},{4,12},{1,5},{9... | collective-permute-start | bytes 1081352 | tf_op jit(solution)/shard_map/ppermute | solution.py:70
  53.8 30.6 %collective-permute-start.1 = (bf16[128,2048]{1,0:T(8,128)(2,1)S(1)}, bf16[128,2048]{1,0:T(8,128)(2,1)S(1)}, u32[]{:S(2)}, u32[]{:S(2)}) collective-permute-start(bf16[128,2048]{1,0:T(8,128)(2,1)S(1)} %constant_dynamic-update-slice_fusion), channel_id=1, source_target_pairs={{0,2},{1,3},{2,0},{3,1},{4,6},{5,7},{6,4},{7,5},{8,10},{9,11},{10,... | collective-permute-start | bytes 1572872 | tf_op jit(solution)/shard_map/ppermute | solution.py:118
  62.9 11.6 %collective-permute-start.32 = (bf16[704,256]{1,0:T(8,128)(2,1)}, bf16[704,256]{1,0:T(8,128)(2,1)S(1)}, u32[]{:S(2)}, u32[]{:S(2)}) collective-permute-start(bf16[704,256]{1,0:T(8,128)(2,1)} %get-tuple-element.156), channel_id=1, source_target_pairs={{0,8},{8,16},{16,24},{24,28},{28,20},{20,12},{12,4},{4,0},{1,9},{9... | collective-permute-start | bytes 1081352 | tf_op jit(solution)/shard_map/ppermute | solution.py:70
  66.2 19.6 %collective-permute-start.5 = (bf16[576,256]{1,0:T(8,128)(2,1)}, bf16[576,256]{1,0:T(8,128)(2,1)S(1)}, u32[]{:S(2)}, u32[]{:S(2)}) collective-permute-start(bf16[576,256]{1,0:T(8,128)(2,1)} %collective-permute-done.3), channel_id=1, source_target_pairs={{0,8},{8,16},{16,24},{24,28},{28,20},{20,12},{12,4},{4,0},{1,9},{9... | collective-permute-start | bytes 884744 | tf_op jit(solution)/shard_map/ppermute | solution.py:70
  68.5 12.8 %collective-permute-start.15 = (bf16[320,256]{1,0:T(8,128)(2,1)S(1)}, bf16[320,256]{1,0:T(8,128)(2,1)S(1)}, u32[]{:S(2)}, u32[]{:S(2)}) collective-permute-start(bf16[320,256]{1,0:T(8,128)(2,1)S(1)} %collective-permute-done.13), channel_id=1, source_target_pairs={{0,8},{8,16},{16,24},{24,28},{28,20},{20,12},{12,4},{4,0},{1,9},{9... | collective-permute-start | bytes 491528 | tf_op jit(solution)/shard_map/ppermute | solution.py:70
  74.5 12.9 %collective-permute-start.6 = (bf16[576,256]{1,0:T(8,128)(2,1)}, bf16[576,256]{1,0:T(8,128)(2,1)S(1)}, u32[]{:S(2)}, u32[]{:S(2)}) collective-permute-start(bf16[576,256]{1,0:T(8,128)(2,1)} %collective-permute-done.4), channel_id=1, source_target_pairs={{0,4},{8,0},{16,8},{24,16},{28,24},{20,28},{12,20},{4,12},{1,5},{9... | collective-permute-start | bytes 884744 | tf_op jit(solution)/shard_map/ppermute | solution.py:70
  84.4 24.9 %collective-permute-start = (bf16[128,2048]{1,0:T(8,128)(2,1)S(1)}, bf16[128,2048]{1,0:T(8,128)(2,1)S(1)}, u32[]{:S(2)}, u32[]{:S(2)}) collective-permute-start(bf16[128,2048]{1,0:T(8,128)(2,1)S(1)} %constant_dynamic-update-slice_fusion), channel_id=1, source_target_pairs={{0,1},{1,0},{2,3},{3,2},{4,5},{5,4},{6,7},{7,6},{8,9},{9,8},{10,11... | collective-permute-start | bytes 1572872 | tf_op jit(solution)/shard_map/ppermute | solution.py:118
  84.4 53.7 %collective-permute-start.33 = (bf16[704,256]{1,0:T(8,128)(2,1)}, bf16[704,256]{1,0:T(8,128)(2,1)}, u32[]{:S(2)}, u32[]{:S(2)}) collective-permute-start(bf16[704,256]{1,0:T(8,128)(2,1)} %get-tuple-element.156), channel_id=1, source_target_pairs={{0,4},{8,0},{16,8},{24,16},{28,24},{20,28},{12,20},{4,12},{1,5},{9... | collective-permute-start | bytes 1081352 | tf_op jit(solution)/shard_map/ppermute | solution.py:70
  85.8 25.2 %collective-permute-start.2 = (bf16[128,2048]{1,0:T(8,128)(2,1)S(1)}, bf16[128,2048]{1,0:T(8,128)(2,1)S(1)}, u32[]{:S(2)}, u32[]{:S(2)}) collective-permute-start(bf16[128,2048]{1,0:T(8,128)(2,1)S(1)} %collective-permute-done.1), channel_id=1, source_target_pairs={{0,1},{1,0},{2,3},{3,2},{4,5},{5,4},{6,7},{7,6},{8,9},{9,8},{10,11... | collective-permute-start | bytes 1572872 | tf_op jit(solution)/shard_map/ppermute | solution.py:118
  85.8 16.5 %collective-permute-start.7 = (bf16[576,256]{1,0:T(8,128)(2,1)S(1)}, bf16[576,256]{1,0:T(8,128)(2,1)S(1)}, u32[]{:S(2)}, u32[]{:S(2)}) collective-permute-start(bf16[576,256]{1,0:T(8,128)(2,1)S(1)} %collective-permute-done.5), channel_id=1, source_target_pairs={{0,8},{8,16},{16,24},{24,28},{28,20},{20,12},{12,4},{4,0},{1,9},{9... | collective-permute-start | bytes 884744 | tf_op jit(solution)/shard_map/ppermute | solution.py:70
  87.4 14.4 %collective-permute-start.8 = (bf16[576,256]{1,0:T(8,128)(2,1)S(1)}, bf16[576,256]{1,0:T(8,128)(2,1)S(1)}, u32[]{:S(2)}, u32[]{:S(2)}) collective-permute-start(bf16[576,256]{1,0:T(8,128)(2,1)S(1)} %collective-permute-done.6), channel_id=1, source_target_pairs={{0,4},{8,0},{16,8},{24,16},{28,24},{20,28},{12,20},{4,12},{1,5},{9... | collective-permute-start | bytes 884744 | tf_op jit(solution)/shard_map/ppermute | solution.py:70
  107.3 32.1 %collective-permute-start.24 = (bf16[704,256]{1,0:T(8,128)(2,1)}, bf16[704,256]{1,0:T(8,128)(2,1)}, u32[]{:S(2)}, u32[]{:S(2)}) collective-permute-start(bf16[704,256]{1,0:T(8,128)(2,1)} %get-tuple-element.65), channel_id=1, source_target_pairs={{0,8},{8,16},{16,24},{24,28},{28,20},{20,12},{12,4},{4,0},{1,9},{9... | collective-permute-start | bytes 1081352 | tf_op jit(solution)/shard_map/ppermute | solution.py:70
  108.8 33.2 %collective-permute-start.25 = (bf16[704,256]{1,0:T(8,128)(2,1)}, bf16[704,256]{1,0:T(8,128)(2,1)}, u32[]{:S(2)}, u32[]{:S(2)}) collective-permute-start(bf16[704,256]{1,0:T(8,128)(2,1)} %get-tuple-element.65), channel_id=1, source_target_pairs={{0,4},{8,0},{16,8},{24,16},{28,24},{20,28},{12,20},{4,12},{1,5},{9... | collective-permute-start | bytes 1081352 | tf_op jit(solution)/shard_map/ppermute | solution.py:70
  109.4 34.2 %collective-permute-start.42 = (bf16[704,256]{1,0:T(8,128)(2,1)}, bf16[704,256]{1,0:T(8,128)(2,1)}, u32[]{:S(2)}, u32[]{:S(2)}) collective-permute-start(bf16[704,256]{1,0:T(8,128)(2,1)} %collective-permute-done.40), channel_id=1, source_target_pairs={{0,8},{8,16},{16,24},{24,28},{28,20},{20,12},{12,4},{4,0},{1,9},{9... | collective-permute-start | bytes 1081352 | tf_op jit(solution)/shard_map/ppermute | solution.py:70
  111.0 35.3 %collective-permute-start.43 = (bf16[704,256]{1,0:T(8,128)(2,1)}, bf16[704,256]{1,0:T(8,128)(2,1)}, u32[]{:S(2)}, u32[]{:S(2)}) collective-permute-start(bf16[704,256]{1,0:T(8,128)(2,1)} %collective-permute-done.41), channel_id=1, source_target_pairs={{0,4},{8,0},{16,8},{24,16},{28,24},{20,28},{12,20},{4,12},{1,5},{9... | collective-permute-start | bytes 1081352 | tf_op jit(solution)/shard_map/ppermute | solution.py:70
  138.1 23.9 %collective-permute-start.19 = (bf16[256,2048]{1,0:T(8,128)(2,1)S(1)}, bf16[256,2048]{1,0:T(8,128)(2,1)S(1)}, u32[]{:S(2)}, u32[]{:S(2)}) collective-permute-start(bf16[256,2048]{1,0:T(8,128)(2,1)S(1)} %pad_maximum_fusion.4), channel_id=1, source_target_pairs={{0,1},{1,0},{2,3},{3,2},{4,5},{5,4},{6,7},{7,6},{8,9},{9,8},{10,11... | collective-permute-start | bytes 3145736 | tf_op jit(solution)/shard_map/ppermute | solution.py:118
  139.4 11.3 %collective-permute-start.34 = (bf16[704,256]{1,0:T(8,128)(2,1)S(1)}, bf16[704,256]{1,0:T(8,128)(2,1)S(1)}, u32[]{:S(2)}, u32[]{:S(2)}) collective-permute-start(bf16[704,256]{1,0:T(8,128)(2,1)S(1)} %copy-done.36), channel_id=1, source_target_pairs={{0,8},{8,16},{16,24},{24,28},{28,20},{20,12},{12,4},{4,0},{1,9},{9... | collective-permute-start | bytes 1081352 | tf_op jit(solution)/shard_map/ppermute | solution.py:70
  142.1 11.5 %collective-permute-start.35 = (bf16[704,256]{1,0:T(8,128)(2,1)}, bf16[704,256]{1,0:T(8,128)(2,1)S(1)}, u32[]{:S(2)}, u32[]{:S(2)}) collective-permute-start(bf16[704,256]{1,0:T(8,128)(2,1)} %collective-permute-done.33), channel_id=1, source_target_pairs={{0,4},{8,0},{16,8},{24,16},{28,24},{20,28},{12,20},{4,12},{1,5},{9... | collective-permute-start | bytes 1081352 | tf_op jit(solution)/shard_map/ppermute | solution.py:70
  143.6 14.8 %collective-permute-start.26 = (bf16[704,256]{1,0:T(8,128)(2,1)}, bf16[704,256]{1,0:T(8,128)(2,1)S(1)}, u32[]{:S(2)}, u32[]{:S(2)}) collective-permute-start(bf16[704,256]{1,0:T(8,128)(2,1)} %collective-permute-done.24), channel_id=1, source_target_pairs={{0,8},{8,16},{16,24},{24,28},{28,20},{20,12},{12,4},{4,0},{1,9},{9... | collective-permute-start | bytes 1081352 | tf_op jit(solution)/shard_map/ppermute | solution.py:70
  146.3 15.1 %collective-permute-start.27 = (bf16[704,256]{1,0:T(8,128)(2,1)}, bf16[704,256]{1,0:T(8,128)(2,1)S(1)}, u32[]{:S(2)}, u32[]{:S(2)}) collective-permute-start(bf16[704,256]{1,0:T(8,128)(2,1)} %collective-permute-done.25), channel_id=1, source_target_pairs={{0,4},{8,0},{16,8},{24,16},{28,24},{20,28},{12,20},{4,12},{1,5},{9... | collective-permute-start | bytes 1081352 | tf_op jit(solution)/shard_map/ppermute | solution.py:70
  150.7 19.0 %collective-permute-start.44 = (bf16[704,256]{1,0:T(8,128)(2,1)}, bf16[704,256]{1,0:T(8,128)(2,1)S(1)}, u32[]{:S(2)}, u32[]{:S(2)}) collective-permute-start(bf16[704,256]{1,0:T(8,128)(2,1)} %collective-permute-done.42), channel_id=1, source_target_pairs={{0,8},{8,16},{16,24},{24,28},{28,20},{20,12},{12,4},{4,0},{1,9},{9... | collective-permute-start | bytes 1081352 | tf_op jit(solution)/shard_map/ppermute | solution.py:70
  153.6 15.4 %collective-permute-start.45 = (bf16[704,256]{1,0:T(8,128)(2,1)}, bf16[704,256]{1,0:T(8,128)(2,1)S(1)}, u32[]{:S(2)}, u32[]{:S(2)}) collective-permute-start(bf16[704,256]{1,0:T(8,128)(2,1)} %collective-permute-done.43), channel_id=1, source_target_pairs={{0,4},{8,0},{16,8},{24,16},{28,24},{20,28},{12,20},{4,12},{1,5},{9... | collective-permute-start | bytes 1081352 | tf_op jit(solution)/shard_map/ppermute | solution.py:70
  158.4 17.9 %collective-permute-start.36 = (bf16[704,256]{1,0:T(8,128)(2,1)S(1)}, bf16[704,256]{1,0:T(8,128)(2,1)S(1)}, u32[]{:S(2)}, u32[]{:S(2)}) collective-permute-start(bf16[704,256]{1,0:T(8,128)(2,1)S(1)} %collective-permute-done.34), channel_id=1, source_target_pairs={{0,8},{8,16},{16,24},{24,28},{28,20},{20,12},{12,4},{4,0},{1,9},{9... | collective-permute-start | bytes 1081352 | tf_op jit(solution)/shard_map/ppermute | solution.py:70
  161.3 14.6 %collective-permute-start.37 = (bf16[704,256]{1,0:T(8,128)(2,1)S(1)}, bf16[704,256]{1,0:T(8,128)(2,1)S(1)}, u32[]{:S(2)}, u32[]{:S(2)}) collective-permute-start(bf16[704,256]{1,0:T(8,128)(2,1)S(1)} %collective-permute-done.35), channel_id=1, source_target_pairs={{0,4},{8,0},{16,8},{24,16},{28,24},{20,28},{12,20},{4,12},{1,5},{9... | collective-permute-start | bytes 1081352 | tf_op jit(solution)/shard_map/ppermute | solution.py:70
  162.1 15.8 %collective-permute-start.20 = (bf16[128,2048]{1,0:T(8,128)(2,1)S(1)}, bf16[128,2048]{1,0:T(8,128)(2,1)S(1)}, u32[]{:S(2)}, u32[]{:S(2)}) collective-permute-start(bf16[128,2048]{1,0:T(8,128)(2,1)S(1)} %fusion.19), channel_id=1, source_target_pairs={{0,2},{1,3},{2,0},{3,1},{4,6},{5,7},{6,4},{7,5},{8,10},{9,11},{10,... | collective-permute-start | bytes 1572872 | tf_op jit(solution)/shard_map/ppermute | solution.py:118
  169.0 16.3 %collective-permute-start.51 = (bf16[128,2048]{1,0:T(8,128)(2,1)S(1)}, bf16[128,2048]{1,0:T(8,128)(2,1)S(1)}, u32[]{:S(2)}, u32[]{:S(2)}) collective-permute-start(bf16[128,2048]{1,0:T(8,128)(2,1)S(1)} %copy-done.20), channel_id=1, source_target_pairs={{0,2},{1,3},{2,0},{3,1},{4,6},{5,7},{6,4},{7,5},{8,10},{9,11},{10,... | collective-permute-start | bytes 1572872 | tf_op jit(solution)/shard_map/ppermute | solution.py:118
  169.6 15.7 %collective-permute-start.28 = (bf16[704,256]{1,0:T(8,128)(2,1)S(1)}, bf16[704,256]{1,0:T(8,128)(2,1)S(1)}, u32[]{:S(2)}, u32[]{:S(2)}) collective-permute-start(bf16[704,256]{1,0:T(8,128)(2,1)S(1)} %collective-permute-done.26), channel_id=1, source_target_pairs={{0,8},{8,16},{16,24},{24,28},{28,20},{20,12},{12,4},{4,0},{1,9},{9... | collective-permute-start | bytes 1081352 | tf_op jit(solution)/shard_map/ppermute | solution.py:70
  175.9 11.3 %collective-permute-start.29 = (bf16[704,256]{1,0:T(8,128)(2,1)S(1)}, bf16[704,256]{1,0:T(8,128)(2,1)S(1)}, u32[]{:S(2)}, u32[]{:S(2)}) collective-permute-start(bf16[704,256]{1,0:T(8,128)(2,1)S(1)} %collective-permute-done.27), channel_id=1, source_target_pairs={{0,4},{8,0},{16,8},{24,16},{28,24},{20,28},{12,20},{4,12},{1,5},{9... | collective-permute-start | bytes 1081352 | tf_op jit(solution)/shard_map/ppermute | solution.py:70
  176.4 13.6 %collective-permute-start.47 = (bf16[352,256]{1,0:T(8,128)(2,1)S(1)}, bf16[352,256]{1,0:T(8,128)(2,1)S(1)}, u32[]{:S(2)}, u32[]{:S(2)}) collective-permute-start(bf16[352,256]{1,0:T(8,128)(2,1)S(1)} %slice.707), channel_id=1, source_target_pairs={{0,4},{8,0},{16,8},{24,16},{28,24},{20,28},{12,20},{4,12},{1,5},{9... | collective-permute-start | bytes 540680 | tf_op jit(solution)/shard_map/ppermute | solution.py:70
  177.9 13.7 %collective-permute-start.46 = (bf16[352,256]{1,0:T(8,128)(2,1)S(1)}, bf16[352,256]{1,0:T(8,128)(2,1)S(1)}, u32[]{:S(2)}, u32[]{:S(2)}) collective-permute-start(bf16[352,256]{1,0:T(8,128)(2,1)S(1)} %slice.706), channel_id=1, source_target_pairs={{0,8},{8,16},{16,24},{24,28},{28,20},{20,12},{12,4},{4,0},{1,9},{9... | collective-permute-start | bytes 540680 | tf_op jit(solution)/shard_map/ppermute | solution.py:70
  185.3 17.4 %collective-permute-start.50 = (bf16[128,2048]{1,0:T(8,128)(2,1)S(1)}, bf16[128,2048]{1,0:T(8,128)(2,1)S(1)}, u32[]{:S(2)}, u32[]{:S(2)}) collective-permute-start(bf16[128,2048]{1,0:T(8,128)(2,1)S(1)} %copy-done.20), channel_id=1, source_target_pairs={{0,1},{1,0},{2,3},{3,2},{4,5},{5,4},{6,7},{7,6},{8,9},{9,8},{10,11... | collective-permute-start | bytes 1572872 | tf_op jit(solution)/shard_map/ppermute | solution.py:118
  185.3 17.4 %collective-permute-start.52 = (bf16[128,2048]{1,0:T(8,128)(2,1)S(1)}, bf16[128,2048]{1,0:T(8,128)(2,1)S(1)}, u32[]{:S(2)}, u32[]{:S(2)}) collective-permute-start(bf16[128,2048]{1,0:T(8,128)(2,1)S(1)} %collective-permute-done.51), channel_id=1, source_target_pairs={{0,1},{1,0},{2,3},{3,2},{4,5},{5,4},{6,7},{7,6},{8,9},{9,8},{10,11... | collective-permute-start | bytes 1572872 | tf_op jit(solution)/shard_map/ppermute | solution.py:118
  191.6 11.1 %collective-permute-start.22 = (bf16[128,2048]{1,0:T(8,128)(2,1)S(1)}, bf16[128,2048]{1,0:T(8,128)(2,1)S(1)}, u32[]{:S(2)}, u32[]{:S(2)}) collective-permute-start(bf16[128,2048]{1,0:T(8,128)(2,1)S(1)} %multiply_convert_fusion.4), channel_id=1, source_target_pairs={{0,2},{1,3},{2,0},{3,1},{4,6},{5,7},{6,4},{7,5},{8,10},{9,11},{10,... | collective-permute-start | bytes 1572872 | tf_op jit(solution)/shard_map/ppermute | solution.py:118
  213.6 69.4 %collective-permute-start.53 = (bf16[256,2048]{1,0:T(8,128)(2,1)S(1)}, bf16[256,2048]{1,0:T(8,128)(2,1)S(1)}, u32[]{:S(2)}, u32[]{:S(2)}) collective-permute-start(bf16[256,2048]{1,0:T(8,128)(2,1)S(1)} %pad_maximum_fusion.6), channel_id=1, source_target_pairs={{0,1},{1,0},{2,3},{3,2},{4,5},{5,4},{6,7},{7,6},{8,9},{9,8},{10,11... | collective-permute-start | bytes 3145736 | tf_op jit(solution)/shard_map/ppermute | solution.py:118
  219.3 10.8 %collective-permute-start.80 = (bf16[352,256]{1,0:T(8,128)(2,1)S(1)}, bf16[352,256]{1,0:T(8,128)(2,1)S(1)}, u32[]{:S(2)}, u32[]{:S(2)}) collective-permute-start(bf16[352,256]{1,0:T(8,128)(2,1)S(1)} %get-tuple-element.98), channel_id=1, source_target_pairs={{0,4},{8,0},{16,8},{24,16},{28,24},{20,28},{12,20},{4,12},{1,5},{9... | collective-permute-start | bytes 540680 | tf_op jit(solution)/shard_map/ppermute | solution.py:70
  230.8 13.0 %collective-permute-start.77 = (bf16[704,256]{1,0:T(8,128)(2,1)S(1)}, bf16[704,256]{1,0:T(8,128)(2,1)S(1)}, u32[]{:S(2)}, u32[]{:S(2)}) collective-permute-start(bf16[704,256]{1,0:T(8,128)(2,1)S(1)} %pad_maximum_fusion.11), channel_id=1, source_target_pairs={{0,8},{8,16},{16,24},{24,28},{28,20},{20,12},{12,4},{4,0},{1,9},{9... | collective-permute-start | bytes 1081352 | tf_op jit(solution)/shard_map/ppermute | solution.py:70
  232.3 28.5 %collective-permute-start.81 = (bf16[704,256]{1,0:T(8,128)(2,1)S(1)}, bf16[704,256]{1,0:T(8,128)(2,1)S(1)}, u32[]{:S(2)}, u32[]{:S(2)}) collective-permute-start(bf16[704,256]{1,0:T(8,128)(2,1)S(1)} %pad_maximum_fusion.12), channel_id=1, source_target_pairs={{0,4},{8,0},{16,8},{24,16},{28,24},{20,28},{12,20},{4,12},{1,5},{9... | collective-permute-start | bytes 1081352 | tf_op jit(solution)/shard_map/ppermute | solution.py:70
  236.1 15.4 %collective-permute-start.69 = (bf16[704,256]{1,0:T(8,128)(2,1)S(1)}, bf16[704,256]{1,0:T(8,128)(2,1)S(1)}, u32[]{:S(2)}, u32[]{:S(2)}) collective-permute-start(bf16[704,256]{1,0:T(8,128)(2,1)S(1)} %pad_maximum_fusion.9), channel_id=1, source_target_pairs={{0,8},{8,16},{16,24},{24,28},{28,20},{20,12},{12,4},{4,0},{1,9},{9... | collective-permute-start | bytes 1081352 | tf_op jit(solution)/shard_map/ppermute | solution.py:70
  237.6 31.1 %collective-permute-start.73 = (bf16[704,256]{1,0:T(8,128)(2,1)S(1)}, bf16[704,256]{1,0:T(8,128)(2,1)S(1)}, u32[]{:S(2)}, u32[]{:S(2)}) collective-permute-start(bf16[704,256]{1,0:T(8,128)(2,1)S(1)} %pad_maximum_fusion.10), channel_id=1, source_target_pairs={{0,4},{8,0},{16,8},{24,16},{28,24},{20,28},{12,20},{4,12},{1,5},{9... | collective-permute-start | bytes 1081352 | tf_op jit(solution)/shard_map/ppermute | solution.py:70
  243.8 15.4 %collective-permute-start.97 = (bf16[704,256]{1,0:T(8,128)(2,1)S(1)}, bf16[704,256]{1,0:T(8,128)(2,1)S(1)}, u32[]{:S(2)}, u32[]{:S(2)}) collective-permute-start(bf16[704,256]{1,0:T(8,128)(2,1)S(1)} %pad_maximum_fusion.13), channel_id=1, source_target_pairs={{0,8},{8,16},{16,24},{24,28},{28,20},{20,12},{12,4},{4,0},{1,9},{9... | collective-permute-start | bytes 1081352 | tf_op jit(solution)/shard_map/ppermute | solution.py:70
  251.5 15.4 %collective-permute-start.78 = (bf16[704,256]{1,0:T(8,128)(2,1)S(1)}, bf16[704,256]{1,0:T(8,128)(2,1)S(1)}, u32[]{:S(2)}, u32[]{:S(2)}) collective-permute-start(bf16[704,256]{1,0:T(8,128)(2,1)S(1)} %fusion.28), channel_id=1, source_target_pairs={{0,8},{8,16},{16,24},{24,28},{28,20},{20,12},{12,4},{4,0},{1,9},{9... | collective-permute-start | bytes 1081352 | tf_op jit(solution)/shard_map/ppermute | solution.py:70
  259.3 15.4 %collective-permute-start.70 = (bf16[704,256]{1,0:T(8,128)(2,1)S(1)}, bf16[704,256]{1,0:T(8,128)(2,1)S(1)}, u32[]{:S(2)}, u32[]{:S(2)}) collective-permute-start(bf16[704,256]{1,0:T(8,128)(2,1)S(1)} %fusion.33), channel_id=1, source_target_pairs={{0,8},{8,16},{16,24},{24,28},{28,20},{20,12},{12,4},{4,0},{1,9},{9... | collective-permute-start | bytes 1081352 | tf_op jit(solution)/shard_map/ppermute | solution.py:70
  260.9 14.4 %collective-permute-start.101 = (bf16[704,256]{1,0:T(8,128)(2,1)S(1)}, bf16[704,256]{1,0:T(8,128)(2,1)S(1)}, u32[]{:S(2)}, u32[]{:S(2)}) collective-permute-start(bf16[704,256]{1,0:T(8,128)(2,1)S(1)} %pad_maximum_fusion.14), channel_id=1, source_target_pairs={{0,4},{8,0},{16,8},{24,16},{28,24},{20,28},{12,20},{4,12},{1,5},{9... | collective-permute-start | bytes 1081352 | tf_op jit(solution)/shard_map/ppermute | solution.py:70
  267.0 15.4 %collective-permute-start.98 = (bf16[704,256]{1,0:T(8,128)(2,1)S(1)}, bf16[704,256]{1,0:T(8,128)(2,1)S(1)}, u32[]{:S(2)}, u32[]{:S(2)}) collective-permute-start(bf16[704,256]{1,0:T(8,128)(2,1)S(1)} %fusion.23), channel_id=1, source_target_pairs={{0,8},{8,16},{16,24},{24,28},{28,20},{20,12},{12,4},{4,0},{1,9},{9... | collective-permute-start | bytes 1081352 | tf_op jit(solution)/shard_map/ppermute | solution.py:70
  268.7 16.1 %collective-permute-start.48 = (bf16[256,2048]{1,0:T(8,128)(2,1)S(1)}, bf16[256,2048]{1,0:T(8,128)(2,1)S(1)}, u32[]{:S(2)}, u32[]{:S(2)}) collective-permute-start(bf16[256,2048]{1,0:T(8,128)(2,1)S(1)} %pad_maximum_fusion.5), channel_id=1, source_target_pairs={{0,1},{1,0},{2,3},{3,2},{4,5},{5,4},{6,7},{7,6},{8,9},{9,8},{10,11... | collective-permute-start | bytes 3145736 | tf_op jit(solution)/shard_map/ppermute | solution.py:118
  275.3 35.2 %collective-permute-start.79 = (bf16[704,256]{1,0:T(8,128)(2,1)S(1)}, bf16[704,256]{1,0:T(8,128)(2,1)S(1)}, u32[]{:S(2)}, u32[]{:S(2)}) collective-permute-start(bf16[704,256]{1,0:T(8,128)(2,1)S(1)} %get-tuple-element.79), channel_id=1, source_target_pairs={{0,8},{8,16},{16,24},{24,28},{28,20},{20,12},{12,4},{4,0},{1,9},{9... | collective-permute-start | bytes 1081352 | tf_op jit(solution)/shard_map/ppermute | solution.py:70
  282.4 11.3 %collective-permute-start.74 = (bf16[704,256]{1,0:T(8,128)(2,1)S(1)}, bf16[704,256]{1,0:T(8,128)(2,1)S(1)}, u32[]{:S(2)}, u32[]{:S(2)}) collective-permute-start(bf16[704,256]{1,0:T(8,128)(2,1)S(1)} %get-tuple-element.84), channel_id=1, source_target_pairs={{0,4},{8,0},{16,8},{24,16},{28,24},{20,28},{12,20},{4,12},{1,5},{9... | collective-permute-start | bytes 1081352 | tf_op jit(solution)/shard_map/ppermute | solution.py:70
  283.1 37.5 %collective-permute-start.71 = (bf16[704,256]{1,0:T(8,128)(2,1)S(1)}, bf16[704,256]{1,0:T(8,128)(2,1)S(1)}, u32[]{:S(2)}, u32[]{:S(2)}) collective-permute-start(bf16[704,256]{1,0:T(8,128)(2,1)S(1)} %get-tuple-element.83), channel_id=1, source_target_pairs={{0,8},{8,16},{16,24},{24,28},{28,20},{20,12},{12,4},{4,0},{1,9},{9... | collective-permute-start | bytes 1081352 | tf_op jit(solution)/shard_map/ppermute | solution.py:70
  284.8 13.4 %collective-permute-start.102 = (bf16[704,256]{1,0:T(8,128)(2,1)S(1)}, bf16[704,256]{1,0:T(8,128)(2,1)S(1)}, u32[]{:S(2)}, u32[]{:S(2)}) collective-permute-start(bf16[704,256]{1,0:T(8,128)(2,1)S(1)} %get-tuple-element.76), channel_id=1, source_target_pairs={{0,4},{8,0},{16,8},{24,16},{28,24},{20,28},{12,20},{4,12},{1,5},{9... | collective-permute-start | bytes 1081352 | tf_op jit(solution)/shard_map/ppermute | solution.py:70
  285.4 12.9 %collective-permute-start.54 = (bf16[128,2048]{1,0:T(8,128)(2,1)S(1)}, bf16[128,2048]{1,0:T(8,128)(2,1)S(1)}, u32[]{:S(2)}, u32[]{:S(2)}) collective-permute-start(bf16[128,2048]{1,0:T(8,128)(2,1)S(1)} %fusion.13), channel_id=1, source_target_pairs={{0,2},{1,3},{2,0},{3,1},{4,6},{5,7},{6,4},{7,5},{8,10},{9,11},{10,... | collective-permute-start | bytes 1572872 | tf_op jit(solution)/shard_map/ppermute | solution.py:118
  293.7 17.3 %collective-permute-start.99 = (bf16[704,256]{1,0:T(8,128)(2,1)S(1)}, bf16[704,256]{1,0:T(8,128)(2,1)S(1)}, u32[]{:S(2)}, u32[]{:S(2)}) collective-permute-start(bf16[704,256]{1,0:T(8,128)(2,1)S(1)} %get-tuple-element.75), channel_id=1, source_target_pairs={{0,8},{8,16},{16,24},{24,28},{28,20},{20,12},{12,4},{4,0},{1,9},{9... | collective-permute-start | bytes 1081352 | tf_op jit(solution)/shard_map/ppermute | solution.py:70
  298.4 13.7 %collective-permute-start.103 = (bf16[704,256]{1,0:T(8,128)(2,1)S(1)}, bf16[704,256]{1,0:T(8,128)(2,1)S(1)}, u32[]{:S(2)}, u32[]{:S(2)}) collective-permute-start(bf16[704,256]{1,0:T(8,128)(2,1)S(1)} %fusion.22), channel_id=1, source_target_pairs={{0,4},{8,0},{16,8},{24,16},{28,24},{20,28},{12,20},{4,12},{1,5},{9... | collective-permute-start | bytes 1081352 | tf_op jit(solution)/shard_map/ppermute | solution.py:70
  311.1 12.0 %collective-permute-start.75 = (bf16[704,256]{1,0:T(8,128)(2,1)S(1)}, bf16[704,256]{1,0:T(8,128)(2,1)S(1)}, u32[]{:S(2)}, u32[]{:S(2)}) collective-permute-start(bf16[704,256]{1,0:T(8,128)(2,1)S(1)} %fusion.32), channel_id=1, source_target_pairs={{0,4},{8,0},{16,8},{24,16},{28,24},{20,28},{12,20},{4,12},{1,5},{9... | collective-permute-start | bytes 1081352 | tf_op jit(solution)/shard_map/ppermute | solution.py:70
  312.1 13.0 %collective-permute-start.55 = (bf16[128,2048]{1,0:T(8,128)(2,1)S(1)}, bf16[128,2048]{1,0:T(8,128)(2,1)S(1)}, u32[]{:S(2)}, u32[]{:S(2)}) collective-permute-start(bf16[128,2048]{1,0:T(8,128)(2,1)S(1)} %get-tuple-element.62), channel_id=1, source_target_pairs={{0,1},{1,0},{2,3},{3,2},{4,5},{5,4},{6,7},{7,6},{8,9},{9,8},{10,11... | collective-permute-start | bytes 1572872 | tf_op jit(solution)/shard_map/ppermute | solution.py:118
  360.2 81.6 %collective-permute-start.58 = (bf16[256,2048]{1,0:T(8,128)(2,1)}, bf16[256,2048]{1,0:T(8,128)(2,1)S(1)}, u32[]{:S(2)}, u32[]{:S(2)}) collective-permute-start(bf16[256,2048]{1,0:T(8,128)(2,1)} %pad_maximum_fusion.7), channel_id=1, source_target_pairs={{0,1},{1,0},{2,3},{3,2},{4,5},{5,4},{6,7},{7,6},{8,9},{9,8},{10,11... | collective-permute-start | bytes 3145736 | tf_op jit(solution)/shard_map/ppermute | solution.py:118
  376.8 52.1 %collective-permute-start.65 = (bf16[576,256]{1,0:T(8,128)(2,1)S(1)}, bf16[576,256]{1,0:T(8,128)(2,1)S(1)}, u32[]{:S(2)}, u32[]{:S(2)}) collective-permute-start(bf16[576,256]{1,0:T(8,128)(2,1)S(1)} %pad_maximum_fusion.21), channel_id=1, source_target_pairs={{0,4},{8,0},{16,8},{24,16},{28,24},{20,28},{12,20},{4,12},{1,5},{9... | collective-permute-start | bytes 884744 | tf_op jit(solution)/shard_map/ppermute | solution.py:70
  381.7 44.9 %collective-permute-start.94 = (bf16[320,256]{1,0:T(8,128)(2,1)S(1)}, bf16[320,256]{1,0:T(8,128)(2,1)S(1)}, u32[]{:S(2)}, u32[]{:S(2)}) collective-permute-start(bf16[320,256]{1,0:T(8,128)(2,1)S(1)} %get-tuple-element.109), channel_id=1, source_target_pairs={{0,4},{8,0},{16,8},{24,16},{28,24},{20,28},{12,20},{4,12},{1,5},{9... | collective-permute-start | bytes 491528 | tf_op jit(solution)/shard_map/ppermute | solution.py:70
  385.7 43.3 %collective-permute-start.62 = (bf16[576,256]{1,0:T(8,128)(2,1)S(1)}, bf16[576,256]{1,0:T(8,128)(2,1)S(1)}, u32[]{:S(2)}, u32[]{:S(2)}) collective-permute-start(bf16[576,256]{1,0:T(8,128)(2,1)S(1)} %fusion.49), channel_id=1, source_target_pairs={{0,8},{8,16},{16,24},{24,28},{28,20},{20,12},{12,4},{4,0},{1,9},{9... | collective-permute-start | bytes 884744 | tf_op jit(solution)/shard_map/ppermute | solution.py:70
  441.9 12.6 %collective-permute-start.59 = (bf16[128,2048]{1,0:T(8,128)(2,1)S(1)}, bf16[128,2048]{1,0:T(8,128)(2,1)S(1)}, u32[]{:S(2)}, u32[]{:S(2)}) collective-permute-start(bf16[128,2048]{1,0:T(8,128)(2,1)S(1)} %fusion.11), channel_id=1, source_target_pairs={{0,2},{1,3},{2,0},{3,1},{4,6},{5,7},{6,4},{7,5},{8,10},{9,11},{10,... | collective-permute-start | bytes 1572872 | tf_op jit(solution)/shard_map/ppermute | solution.py:118
  (124 other events, 975.0 us)
